TPU v7x, 256 devices: a whole 4x4x8 slice. The times are simulated.
256 devices in a mesh: dp: 8 (over z_lo, y), ctx: 32 (over x, z_hi, core).
Axes of the slice: x: 4, y: 4, z: 8 (z_hi: 4, z_lo: 2; z = z_hi * 2 + z_lo), core: 2. Of those that a mesh axis runs over, the one named last changes fastest.
Arguments:
- query_in: bfloat16 [8, 4096, 1024], P('dp', 'ctx'), may hold values from -170 to 170
- key_in: bfloat16 [8, 4096, 1024], P('dp', 'ctx'), may hold values from -4.6 to 4.6
- value_in: bfloat16 [8, 4096, 1024], P('dp', 'ctx'), may hold values from -6 to 6
- residual: bfloat16 [8, 4096, 1920], P('dp', 'ctx'), may hold values from -6 to 6
- w_out: bfloat16 [1024, 1920], replicated, may hold values from -0.1875 to 0.1875
- norm_gain: float32 [1920], replicated, may hold values from 0.25 to 1.75
- short_taps: float32 [3, 7, 1920], replicated, may hold values from -4 to 4
- filters: bfloat16 [15, 128], replicated, may hold values from -1.25 to 1.25
- skip_gain: float32 [1920], replicated, may hold values from -1 to 1
- cotangent: bfloat16 [8, 4096, 1920], P('dp', 'ctx'), may hold values from -6 to 6
Outputs:
- layer_out: bfloat16 [8, 4096, 1920], P('dp', 'ctx')
- grad_residual: bfloat16 [8, 4096, 1920], P('dp', 'ctx')
- grad_query: bfloat16 [8, 4096, 1024], P('dp', 'ctx')
- grad_key: bfloat16 [8, 4096, 1024], P('dp', 'ctx')
- grad_value: bfloat16 [8, 4096, 1024], P('dp', 'ctx')
- grad_weight: float32 [1024, 1920], P('dp', 'ctx')
- grad_gain: float32 [1920], replicated
- grad_taps: float32 [3, 7, 1920], replicated
- grad_filters: float32 [15, 128], replicated
- grad_skip: float32 [1920], replicated
All inputs are finite; a program needn't handle non-finite values.
Results may differ from a plain program's by a relative error of at most 0.029.
Values may be sent and summed in bfloat16 or wider, within the bound.
No kernel may reach another device: no remote copies, remote signals or barrier semaphores. Data moves between devices by JAX's collectives and lax.ppermute only.
A program may use at most 128 MiB of HBM per device.

v0:
```python
import jax
import jax.numpy as jnp
from jax import lax
from jax.experimental import pallas as pl
from jax.experimental.pallas import tpu as pltpu
from jax.sharding import Mesh, PartitionSpec as P

D = 1920
HEADS = 8
HDIM = 128
SHORT = 7
LONG = 128
FCH = 128
FILTERS = 15
AD = HEADS * HDIM
FAR = 16
SMALL = 3 * SHORT + 3
CHUNK = 16
SPAN = 4 * LONG

DP_AXES = ("zl", "y")
CTX_AXES = ("xa", "xb", "zh", "c")
HEAD_AXES = ("xa", "zh")


def from_behind(x, by):
    peers = lax.axis_size(CTX_AXES)
    pairs = [(i, i + by) for i in range(peers) if 0 <= i + by < peers]
    return lax.ppermute(x, CTX_AXES, pairs)


def swap(x, axis):
    return lax.ppermute(x, axis, [(0, 1), (1, 0)])


def exchange(x, axes):
    return lax.all_to_all(x, axes, split_axis=0, concat_axis=0, tiled=True)


def toeplitz_kernel(forward_rows, backward_rows, forward_matrix, backward_matrix):
    for g in range(FILTERS):
        for rows, matrix in ((forward_rows, forward_matrix), (backward_rows, backward_matrix)):
            spread = jnp.broadcast_to(rows[g : g + 1, :], (LONG, 2 * LONG))
            matrix[g] = pltpu.roll(spread, 0, 1, stride=1, stride_axis=0).astype(jnp.bfloat16)


def toeplitz(filters):
    taps = filters.astype(jnp.float32)
    gap = jnp.zeros((FILTERS, LONG), jnp.float32)
    forward_rows = jnp.concatenate([gap[:, :1], taps[:, ::-1], gap[:, 1:]], axis=1)
    backward_rows = jnp.concatenate([taps, gap], axis=1)
    shape = jax.ShapeDtypeStruct((FILTERS, LONG, 2 * LONG), jnp.bfloat16)
    return pl.pallas_call(
        toeplitz_kernel,
        out_shape=[shape, shape],
        compiler_params=pltpu.CompilerParams(vmem_limit_bytes=16 * 1024 * 1024),
        cost_estimate=pl.CostEstimate(flops=4000000, bytes_accessed=2000000, transcendentals=0),
    )(forward_rows, backward_rows)


def turn_matrix(kind):
    first = lax.broadcasted_iota(jnp.int32, (LONG, LONG), 0)
    second = lax.broadcasted_iota(jnp.int32, (LONG, LONG), 1)
    return (first + second == LONG - 1).astype(kind)


def hyena_kernel(
    prev_far,
    prev,
    own,
    following,
    following_far,
    x_all,
    cot_all,
    cot_next,
    cot_far,
    inv_rms,
    taps,
    gain,
    skip,
    forward_matrix,
    backward_matrix,
    layer_out,
    grad_residual,
    small,
    ext,
    cot_ext,
    prod,
    mix,
    stream,
    mixed,
    grad_prod,
    grad_stream,
    scaled_all,
    row_sum,
    reversed_sums,
):
    group = pl.program_id(0)
    groups = pl.num_programs(0)
    f32 = jnp.float32
    low = jnp.bfloat16
    edge = LONG + FAR
    columns = pl.ds(pl.multiple_of(group * FCH, FCH), FCH)

    @pl.when(group == 0)
    def _():
        prod[LONG + edge :, :] = jnp.zeros((LONG - FAR, FCH), low)
        mix[2 * LONG + FAR :, :] = jnp.zeros((LONG - FAR, FCH), low)
        row_sum[...] = jnp.zeros_like(row_sum)
        reversed_sums[...] = jnp.zeros_like(reversed_sums)
        small[groups] = jnp.zeros((SMALL, FCH), f32)

    ext[0:FAR, :] = prev_far[...].astype(f32)
    ext[FAR:edge, :] = prev[...].astype(f32)
    ext[edge : edge + LONG, :] = own[...].astype(f32)
    ext[edge + LONG : edge + 2 * LONG, :] = following[...].astype(f32)
    ext[edge + 2 * LONG :, :] = following_far[...].astype(f32)
    cot_ext[0:LONG, :] = cot_all[:, columns].astype(f32)
    cot_ext[LONG : 2 * LONG, :] = cot_next[...].astype(f32)
    cot_ext[2 * LONG :, :] = cot_far[...].astype(f32)

    for first in range(-LONG, 2 * LONG + FAR, CHUNK):
        kinds = []
        if first >= 0:
            kinds.append(0)
        if first < edge:
            kinds += [1, 2]
        sums = {}
        for tap in range(SHORT):
            rows = ext[edge + first - tap : edge + first - tap + CHUNK, :]
            for kind in kinds:
                term = taps[kind * SHORT + tap : kind * SHORT + tap + 1, :] * rows
                sums[kind] = term if tap == 0 else sums[kind] + term
        if 1 in sums:
            prod[LONG + first : LONG + first + CHUNK, :] = (sums[1] * sums[2]).astype(low)
        if 0 in sums:
            mix[first : first + CHUNK, :] = (cot_ext[first : first + CHUNK, :] * sums[0]).astype(
                low
            )
        if 0 <= first < edge:
            for kind in range(3):
                stream[kind, first : first + CHUNK, :] = sums[kind]

    def product_of(matrix, rows):
        return jnp.dot(matrix, rows, preferred_element_type=f32)

    mixed[0:LONG, :] = product_of(forward_matrix[0], prod[0 : 2 * LONG, :])
    mixed[LONG:, :] = product_of(forward_matrix[0, 0:FAR, :], prod[LONG:, :])
    grad_prod[0:LONG, :] = product_of(backward_matrix[0], mix[0 : 2 * LONG, :])
    grad_prod[LONG:, :] = product_of(backward_matrix[0, 0:FAR, :], mix[LONG:, :])
    turned = product_of(turn_matrix(low), mix[0:LONG, :]).astype(low)
    table = lax.dot_general(
        turned, prod[0 : 2 * LONG, :], (((1,), (1,)), ((), ())), preferred_element_type=f32
    )
    table = pltpu.roll(table, 0, 1, stride=1, stride_axis=0)
    diagonals = jnp.sum(table[:, LONG:], axis=0, keepdims=True)
    reversed_sums[pl.ds(group, 1), :] = diagonals

    skip_row = skip[...]
    skip_sum = jnp.zeros((8, FCH), f32)
    for first in range(0, edge, CHUNK):
        rows = slice(first, first + CHUNK)
        prod_rows = prod[LONG + first : LONG + first + CHUNK, :].astype(f32)
        mix_rows = mix[rows, :].astype(f32)
        mixed_rows = mixed[rows, :] + skip_row * prod_rows
        grad_rows = grad_prod[rows, :] + skip_row * mix_rows
        grad_stream[0, rows, :] = cot_ext[rows, :] * mixed_rows
        grad_stream[1, rows, :] = grad_rows * stream[2, rows, :]
        grad_stream[2, rows, :] = grad_rows * stream[1, rows, :]
        if first < LONG:
            x_rows = x_all[rows, columns].astype(f32)
            layer_out[rows, :] = (x_rows + stream[0, rows, :] * mixed_rows).astype(low)
            skip_sum = skip_sum + jnp.sum((mix_rows * prod_rows).reshape(-1, 8, FCH), axis=0)

    gain_row = gain[...]
    gain_sum = jnp.zeros((8, FCH), f32)
    tap_sums = [None] * (3 * SHORT)
    for first in range(0, LONG, CHUNK):
        rows = slice(first, first + CHUNK)
        grad_normed = None
        for tap in range(SHORT):
            normed_rows = ext[edge + first - tap : edge + first - tap + CHUNK, :]
            for kind in range(3):
                at = kind * SHORT + tap
                term = taps[at : at + 1, :] * grad_stream[kind, first + tap : first + tap + CHUNK, :]
                grad_normed = term if grad_normed is None else grad_normed + term
                part = jnp.sum(
                    (grad_stream[kind, rows, :] * normed_rows).reshape(-1, 8, FCH), axis=0
                )
                tap_sums[at] = part if first == 0 else tap_sums[at] + part
        x_rows = x_all[rows, columns].astype(f32)
        scaled = grad_normed * gain_row
        scaled_all[group, rows, :] = scaled
        row_sum[rows, :] = row_sum[rows, :] + scaled * x_rows
        gain_sum = gain_sum + jnp.sum(
            (grad_normed * x_rows * inv_rms[rows, :]).reshape(-1, 8, FCH), axis=0
        )
    for at in range(3 * SHORT):
        small[group, at : at + 1, :] = jnp.sum(tap_sums[at], axis=0, keepdims=True)
    small[group, 3 * SHORT : 3 * SHORT + 1, :] = jnp.sum(gain_sum, axis=0, keepdims=True)
    small[group, 3 * SHORT + 1 : 3 * SHORT + 2, :] = jnp.sum(skip_sum, axis=0, keepdims=True)

    @pl.when(group == groups - 1)
    def _():
        filter_sums = jnp.dot(
            reversed_sums[...], turn_matrix(f32), precision=lax.Precision.HIGHEST, preferred_element_type=f32
        )
        for g in range(FILTERS):
            small[g, SMALL - 1 : SMALL, :] = filter_sums[g : g + 1, :]
        scale = inv_rms[...]
        mean = jnp.sum(row_sum[...], axis=1, keepdims=True) * (1.0 / D)
        factor = scale * scale * mean
        for g in range(FILTERS):
            cols = slice(g * FCH, (g + 1) * FCH)
            x_cols = x_all[:, cols].astype(f32)
            grad = cot_all[:, cols].astype(f32) + scale * (scaled_all[g] - x_cols * factor)
            grad_residual[:, cols] = grad.astype(low)


def hyena(normed, sides, x_first, cotangent, cot_sides, inv_rms, taps, gain, skip, matrices):
    rows = x_first.shape[0]
    f32 = jnp.float32

    def part(count):
        return pl.BlockSpec((count, FCH), lambda g: (0, g))

    def whole(shape):
        return pl.BlockSpec(shape, lambda g: (0,) * len(shape))

    per_group = pl.BlockSpec((1, LONG, 2 * LONG), lambda g: (g, 0, 0))
    edge = LONG + FAR
    return pl.pallas_call(
        hyena_kernel,
        grid=(FILTERS,),
        in_specs=[
            part(FAR),
            part(rows),
            part(rows),
            part(rows),
            part(FAR),
            whole((rows, D)),
            whole((rows, D)),
            part(rows),
            part(FAR),
            whole((rows, 1)),
            part(3 * SHORT),
            part(1),
            part(1),
            per_group,
            per_group,
        ],
        out_specs=[
            part(rows),
            whole((rows, D)),
            whole((FILTERS + 1, SMALL, FCH)),
        ],
        out_shape=[
            jax.ShapeDtypeStruct((rows, D), jnp.bfloat16),
            jax.ShapeDtypeStruct((rows, D), jnp.bfloat16),
            jax.ShapeDtypeStruct((FILTERS + 1, SMALL, FCH), f32),
        ],
        scratch_shapes=[
            pltpu.VMEM((3 * LONG + 2 * FAR, FCH), f32),
            pltpu.VMEM((2 * LONG + FAR, FCH), f32),
            pltpu.VMEM((3 * LONG, FCH), jnp.bfloat16),
            pltpu.VMEM((3 * LONG, FCH), jnp.bfloat16),
            pltpu.VMEM((3, edge, FCH), f32),
            pltpu.VMEM((edge, FCH), f32),
            pltpu.VMEM((edge, FCH), f32),
            pltpu.VMEM((3, edge, FCH), f32),
            pltpu.VMEM((FILTERS, LONG, FCH), f32),
            pltpu.VMEM((LONG, FCH), f32),
            pltpu.VMEM((FILTERS + 1, FCH), f32),
        ],
        compiler_params=pltpu.CompilerParams(
            dimension_semantics=("arbitrary",), vmem_limit_bytes=32 * 1024 * 1024
        ),
        cost_estimate=pl.CostEstimate(
            flops=2 * 4 * 1024 * 1024 * 60, bytes_accessed=12 * 1024 * 1024, transcendentals=0
        ),
    )(
        sides[0],
        sides[1],
        normed,
        sides[2],
        sides[3],
        x_first,
        cotangent,
        cot_sides[0],
        cot_sides[1],
        inv_rms,
        taps.reshape(3 * SHORT, D),
        gain.reshape(1, D),
        skip.reshape(1, D),
        matrices[0],
        matrices[1],
    )


def allowed_keys(kind, core):
    keys = lax.broadcasted_iota(jnp.int32, (SPAN, SPAN), 0)
    queries = lax.broadcasted_iota(jnp.int32, (SPAN, SPAN), 1)
    if kind == 0:
        return queries >= keys
    return queries // LONG + core > keys // LONG


def spans_of(half):
    base = 4 * half
    spans = [(base, 0), (base + 2, 1), (base + 1, 2), (base + 3, 2)]
    return spans + [(span, 3) for span in range(base)]


def logits_of(k_rows, q_rows, kind, core):
    logits = lax.dot_general(
        k_rows, q_rows, (((1,), (1,)), ((), ())), preferred_element_type=jnp.float32
    ) * (HDIM**-0.5)
    if kind < 2:
        logits = jnp.where(allowed_keys(kind, core), logits, -jnp.inf)
    return logits


def attend_kernel(place, query, kv, out, log_total, top, total, wide):
    f32 = jnp.float32
    for half in range(2):
        q_rows = query[half * SPAN : (half + 1) * SPAN, :]
        for span, kind in spans_of(half):

            def visit(span=span, kind=kind):
                rows = slice(span * SPAN, (span + 1) * SPAN)
                logits = logits_of(kv[rows, 0:HDIM], q_rows, kind, place[1])
                high = jnp.max(logits, axis=0, keepdims=True)
                if kind > 0:
                    high = jnp.maximum(high, top[...])
                probs = jnp.exp(logits - high)
                part = jnp.sum(probs, axis=0, keepdims=True)
                values = lax.dot_general(
                    kv[rows, HDIM:],
                    probs.astype(jnp.bfloat16),
                    (((0,), (0,)), ((), ())),
                    preferred_element_type=f32,
                )
                if kind > 0:
                    shrink = jnp.exp(top[...] - high)
                    part = part + total[...] * shrink
                    values = values + wide[...] * shrink
                top[...] = high
                total[...] = part
                wide[...] = values

            if kind == 2:
                pl.when(place[0] == 1)(visit)
            else:
                visit()
        columns = slice(half * SPAN, (half + 1) * SPAN)
        out[columns, :] = (wide[...] / total[...]).T.astype(jnp.bfloat16)
        log_total[:, columns] = top[...] + jnp.log(total[...])


def attend(place, query, kv):
    count = query.shape[0]
    return pl.pallas_call(
        attend_kernel,
        in_specs=[
            pl.BlockSpec(memory_space=pltpu.SMEM),
            pl.BlockSpec(memory_space=pltpu.VMEM),
            pl.BlockSpec(memory_space=pltpu.VMEM),
        ],
        out_shape=[
            jax.ShapeDtypeStruct((count, HDIM), jnp.bfloat16),
            jax.ShapeDtypeStruct((1, count), jnp.float32),
        ],
        scratch_shapes=[
            pltpu.VMEM((1, SPAN), jnp.float32),
            pltpu.VMEM((1, SPAN), jnp.float32),
            pltpu.VMEM((HDIM, SPAN), jnp.float32),
        ],
        compiler_params=pltpu.CompilerParams(vmem_limit_bytes=32 * 1024 * 1024),
        cost_estimate=pl.CostEstimate(
            flops=1600000000, bytes_accessed=3000000, transcendentals=3000000
        ),
    )(place, query, kv)


def attend_back_kernel(
    place, query, kv, out, log_total, grad_out, grad_query, same_core, other_core, sums, wide
):
    f32 = jnp.float32
    low = jnp.bfloat16
    scale = HDIM**-0.5
    for half in range(2):
        columns = slice(half * SPAN, (half + 1) * SPAN)
        q_rows = query[columns, :]
        g_rows = grad_out[columns, :]
        both = g_rows.astype(f32) * out[columns, :].astype(f32)
        delta = jnp.sum(both.T, axis=0, keepdims=True)
        log_row = log_total[:, columns]
        for span, kind in spans_of(half):
            rows = slice(span * SPAN, (span + 1) * SPAN)
            fresh = half == 1 and span >= 4 or half == 0

            def visit(rows=rows, kind=kind, fresh=fresh):
                k_rows = kv[rows, 0:HDIM]
                logits = logits_of(k_rows, q_rows, kind, place[1])
                probs = jnp.exp(logits - log_row)
                grad_probs = lax.dot_general(
                    kv[rows, HDIM:],
                    g_rows,
                    (((1,), (1,)), ((), ())),
                    preferred_element_type=f32,
                )
                grad_logits = (probs * (grad_probs - delta)).astype(low)
                grad_k = jnp.dot(grad_logits, q_rows, preferred_element_type=f32)
                grad_v = jnp.dot(probs.astype(low), g_rows, preferred_element_type=f32)
                if fresh:
                    sums[rows, 0:HDIM] = grad_k
                    sums[rows, HDIM:] = grad_v
                else:
                    sums[rows, 0:HDIM] += grad_k
                    sums[rows, HDIM:] += grad_v
                part = lax.dot_general(
                    k_rows, grad_logits, (((0,), (0,)), ((), ())), preferred_element_type=f32
                )
                wide[...] = part if kind == 0 else wide[...] + part

            if kind == 2:
                pl.when(place[0] == 1)(visit)

                @pl.when(place[0] == 0)
                def _(rows=rows):
                    sums[rows, :] = jnp.zeros((SPAN, 2 * HDIM), f32)
            else:
                visit()
        grad_query[columns, :] = (wide[...] * scale).T.astype(low)
    for xa in range(2):
        for cr, target in ((0, same_core), (1, other_core)):
            for xr in range(2):
                span = xa * 4 + cr * 2 + xr
                rows = slice(span * SPAN, (span + 1) * SPAN)
                target[xa, xr, :, 0:HDIM] = (sums[rows, 0:HDIM] * scale).astype(low)
                target[xa, xr, :, HDIM:] = sums[rows, HDIM:].astype(low)


def attend_back(place, query, kv, out, log_total, grad_out):
    vmem = pl.BlockSpec(memory_space=pltpu.VMEM)
    part = jax.ShapeDtypeStruct((2, 2, SPAN, 2 * HDIM), jnp.bfloat16)
    return pl.pallas_call(
        attend_back_kernel,
        in_specs=[pl.BlockSpec(memory_space=pltpu.SMEM)] + [vmem] * 5,
        out_shape=[jax.ShapeDtypeStruct(query.shape, jnp.bfloat16), part, part],
        scratch_shapes=[
            pltpu.VMEM(kv.shape, jnp.float32),
            pltpu.VMEM((HDIM, SPAN), jnp.float32),
        ],
        compiler_params=pltpu.CompilerParams(vmem_limit_bytes=40 * 1024 * 1024),
        cost_estimate=pl.CostEstimate(
            flops=4000000000, bytes_accessed=6000000, transcendentals=3000000
        ),
    )(place, query, kv, out, log_total, grad_out)


def to_heads(rows_in):
    return rows_in.reshape(rows_in.shape[0], HEADS, HDIM).transpose(1, 0, 2)


def from_heads(pieces):
    return pieces.transpose(1, 0, 2).reshape(pieces.shape[1], HEADS * HDIM)


def gather_keys(kv_own):
    rows = kv_own.shape[1]
    wide = jnp.stack([kv_own, swap(kv_own, "xb")])
    both = jnp.stack([wide, swap(wide, "c")])
    both = both.reshape(2, 2, 2, 4, rows, 2 * HDIM).transpose(2, 0, 1, 3, 4, 5)
    return both.reshape(32 * rows, 2 * HDIM)


def scatter_keys(same_core, other_core):
    f32 = jnp.float32
    parts = same_core.astype(f32) + swap(other_core, "c").astype(f32)
    parts = parts[:, 0] + swap(parts[:, 1].astype(jnp.bfloat16), "xb").astype(f32)
    return parts.reshape(8, -1, 2 * HDIM).astype(jnp.bfloat16)


def weight_sum(attention, grad_residual, small_part):
    core = lax.axis_index("c")
    zl = lax.axis_index("zl")
    half = AD // 2
    mine = jnp.where(core == 0, attention[:, :half], attention[:, half:])
    theirs = jnp.where(core == 0, attention[:, half:], attention[:, :half])
    rows_a = jnp.concatenate([mine, swap(theirs, "c")], axis=0)
    rows_g = jnp.concatenate([grad_residual, swap(grad_residual, "c")], axis=0)
    peers = lax.axis_size("y")
    width = half // peers
    pieces = jnp.stack(
        [
            lax.dot_general(
                rows_g,
                rows_a[:, i * width : (i + 1) * width],
                (((0,), (0,)), ((), ())),
                preferred_element_type=jnp.float32,
            ).astype(jnp.bfloat16)
            for i in range(peers)
        ]
    )
    small_rows = small_part.reshape(1, -1, width).astype(jnp.bfloat16)
    small_rows = jnp.broadcast_to(small_rows, (peers,) + small_rows.shape[1:])
    total = exchange(jnp.concatenate([pieces, small_rows], axis=1), "y")
    total = jnp.sum(total.astype(jnp.float32), axis=0)
    small_part = total[D:]
    total = total[:D].astype(jnp.bfloat16).reshape(16, 2, D // 32, width)

    def flip(x, by):
        return lax.ppermute(x, ("zl", "c"), [(i, i ^ by) for i in range(4)])

    small_part = (small_part + flip(small_part, 2)) + (flip(small_part, 1) + flip(small_part, 3))
    small_part = small_part + swap(small_part, "xb")
    halves = (total[:, 0], total[:, 1])
    received = []
    for turn in range(2):
        piece = jnp.where(zl == 0, halves[turn], halves[1 - turn])
        pairs = [(a * 2 + b, b * 2 + (a ^ turn)) for a in range(2) for b in range(2)]
        received.append(lax.ppermute(piece, ("zl", "c"), pairs).astype(jnp.float32))
    total = (received[0] + received[1]).astype(jnp.bfloat16)
    xb = lax.axis_index("xb")
    total = total.reshape(2, 2, 4, D // 32, width)
    mine = jnp.where(xb == 0, total[:, 0], total[:, 1]).astype(jnp.float32)
    theirs = jnp.where(xb == 0, total[:, 1], total[:, 0])
    total = mine + swap(theirs, "xb").astype(jnp.float32)
    return total.astype(jnp.bfloat16).reshape(8, D // 32, width), small_part


def local(
    query_in,
    key_in,
    value_in,
    residual,
    w_out,
    norm_gain,
    short_taps,
    filters,
    skip_gain,
    cotangent,
):
    tok_rows = query_in.shape[1]
    matrices = toeplitz(filters)
    cot_sides = (from_behind(cotangent[0], -1), from_behind(cotangent[0, :FAR], -2))
    kv_send = jnp.concatenate([to_heads(key_in[0]), to_heads(value_in[0])], axis=2)
    kv_own = exchange(kv_send, HEAD_AXES)
    query_rows = exchange(to_heads(query_in[0]), HEAD_AXES).reshape(8 * tok_rows, HDIM)
    kv_all = gather_keys(kv_own)
    query_total = 8 * tok_rows
    place = jnp.stack([lax.axis_index("xb"), lax.axis_index("c")]).astype(jnp.int32)
    head_out, log_total = attend(place, query_rows, kv_all)
    attention = from_heads(exchange(head_out.reshape(8, tok_rows, HDIM), HEAD_AXES))
    x_float = residual[0].astype(jnp.float32) + jnp.dot(
        attention, w_out, preferred_element_type=jnp.float32
    )
    x_first = lax.optimization_barrier(x_float.astype(jnp.bfloat16))
    x_float = x_first.astype(jnp.float32)
    inv_rms = lax.rsqrt(jnp.mean(x_float * x_float, axis=-1, keepdims=True) + 1e-05)
    normed = lax.optimization_barrier((x_float * inv_rms * norm_gain).astype(jnp.bfloat16))
    sides = (
        from_behind(normed[tok_rows - FAR :], 2),
        from_behind(normed, 1),
        from_behind(normed, -1),
        from_behind(normed[:FAR], -2),
    )
    layer_out, grad_residual, small = hyena(
        normed,
        sides,
        x_first,
        cotangent[0],
        cot_sides,
        inv_rms,
        short_taps,
        norm_gain,
        skip_gain,
        matrices,
    )

    grad_attention = jnp.einsum(
        "td,ad->ta", grad_residual, w_out, preferred_element_type=jnp.float32
    ).astype(jnp.bfloat16)
    small_rows = (FILTERS + 1) * SMALL // 8
    small_send = small.reshape(8, small_rows, HDIM).astype(jnp.bfloat16)
    grad_recv = exchange(
        jnp.concatenate([to_heads(grad_attention), small_send], axis=1), HEAD_AXES
    )
    grad_rows_all = grad_recv[:, :tok_rows].reshape(query_total, HDIM)
    small_part = jnp.sum(grad_recv[:, tok_rows:].astype(jnp.float32), axis=0)
    weight_part, small_part = weight_sum(attention, grad_residual, small_part)
    small_high = small_part.reshape(-1, HDIM).astype(jnp.bfloat16)

    grad_query, same_core, other_core = attend_back(
        place, query_rows, kv_all, head_out, log_total, grad_rows_all
    )
    dq_send = grad_query.reshape(8, tok_rows, HDIM)
    dkv = scatter_keys(same_core, other_core)
    dp_rows = weight_part.shape[2] // HDIM
    weight_rows = weight_part.shape[1] * dp_rows
    last_send = jnp.concatenate(
        [
            dq_send,
            dkv[:, :, :HDIM],
            dkv[:, :, HDIM:],
            jnp.broadcast_to(small_high[None], (8,) + small_high.shape),
            weight_part.reshape(8, weight_rows, HDIM),
        ],
        axis=1,
    )
    last = exchange(last_send, HEAD_AXES)
    grad_query = from_heads(last[:, :tok_rows])
    grad_key = from_heads(last[:, tok_rows : 2 * tok_rows])
    grad_value = from_heads(last[:, 2 * tok_rows : 3 * tok_rows])
    at = 3 * tok_rows
    small_back = last[:, at : at + small_rows].astype(jnp.float32)
    small_back = small_back.reshape(FILTERS + 1, SMALL, FCH)[:FILTERS].transpose(1, 0, 2)
    grad_filters = small_back[SMALL - 1]
    small_back = small_back.reshape(SMALL, D)
    grad_weight = jnp.sum(last[:, at + small_rows :].astype(jnp.float32), axis=0)
    grad_weight = grad_weight.reshape(D // 32, -1).T
    return (
        layer_out[None],
        grad_residual[None],
        grad_query[None],
        grad_key[None],
        grad_value[None],
        grad_weight,
        small_back[3 * SHORT],
        small_back[: 3 * SHORT].reshape(3, SHORT, D),
        grad_filters,
        small_back[3 * SHORT + 1],
    )


def solution(mesh):
    sequences = mesh.shape["dp"]
    split = Mesh(
        mesh.devices.reshape(2, sequences // 2, 2, 2, 4, 2), DP_AXES + CTX_AXES
    )
    rows = P(DP_AXES, CTX_AXES, None)
    in_specs = (rows, rows, rows, rows, P(), P(), P(), P(), P(), rows)
    out_specs = (rows, rows, rows, rows, rows, P(DP_AXES, CTX_AXES), P(), P(), P(), P())
    return jax.shard_map(local, mesh=split, in_specs=in_specs, out_specs=out_specs, check_vma=False)
```

profile of v0, /device:TPU:32, one launch (start us, length us, event | category | flops | bytes accessed | tf_op | source)
XLA Modules:
  0.0 259.4 jit_solution(17233484304486213383)
XLA Ops:
  3.0 29.4 %all_to_all.30 = bf16[8,128,256]{1,2,0:T(8,128)(2,1)S(1)} all-to-all(bf16[8,128,256]{1,2,0:T(8,128)(2,1)S(1)} %pad_maximum_fusion.2), channel_id=1, replica_groups=mesh['zl'=2,'y'=4,'xa'=2,'xb'=2,'zh'=4,'c'=2] {'xa','zh'}, dimensions={0} | all-to-all | bytes 1048576 | tf_op jit(solution)/shard_map/all_to_all | solution.py:37
  33.1 10.7 %collective-permute-done = bf16[8,128,256]{1,2,0:T(8,128)(2,1)S(1)} collective-permute-done((bf16[8,128,256]{1,2,0:T(8,128)(2,1)S(1)}, bf16[8,128,256]{1,2,0:T(8,128)(2,1)S(1)}, u32[]{:S(2)}, u32[]{:S(2)}) %collective-permute-start) | collective-permute-done | bytes 524320 | tf_op jit(solution)/shard_map/ppermute | solution.py:33
  45.6 3.7 %all-to-all-start = ((bf16[8,128,128]{2,1,0:T(8,128)(2,1)}), bf16[8,128,128]{2,1,0:T(8,128)(2,1)S(1)}, u32[]{:S(2)}, u32[]{:S(2)}) async-start(bf16[8,128,128]{2,1,0:T(8,128)(2,1)} %bitcast.132), calls=%async_computation | async-start | bytes 524288 | tf_op jit(solution)/shard_map/all_to_all | solution.py:37
  50.8 11.9 %all-to-all-done = bf16[8,128,128]{2,1,0:T(8,128)(2,1)S(1)} async-done(((bf16[8,128,128]{2,1,0:T(8,128)(2,1)}), bf16[8,128,128]{2,1,0:T(8,128)(2,1)S(1)}, u32[]{:S(2)}, u32[]{:S(2)}) %all-to-all-start) | async-done | bytes 262176 | tf_op jit(solution)/shard_map/all_to_all | solution.py:37
  62.7 5.1 %shard_map.177 = (bf16[1024,128]{1,0:T(8,128)(2,1)S(1)}, f32[1,1024]{1,0:T(1,128)S(1)}) custom-call(s32[2]{0:T(128)S(1)} %pad_add_fusion.place, bf16[1024,128]{1,0:T(8,128)(2,1)S(1)} %bitcast.137, bf16[4096,256]{1,0:T(8,128)(2,1)S(1)} %bitcast.135), custom_call_target="tpu_custom_call" | custom-call | flops 1600000000 | bytes 3000000 | tf_op jit(solution)/shard_map/pallas_call | solution.py:362
  68.6 3.4 %all-to-all-start.2 = ((bf16[8,128,128]{1,2,0:T(8,128)(2,1)}), bf16[8,128,128]{1,2,0:T(8,128)(2,1)S(1)}, u32[]{:S(2)}, u32[]{:S(2)}) async-start(bf16[8,128,128]{1,2,0:T(8,128)(2,1)} %copy.116), calls=%async_computation.2 | async-start | bytes 524288 | tf_op jit(solution)/shard_map/all_to_all | solution.py:37
  78.3 8.0 %all-to-all-done.2 = bf16[8,128,128]{1,2,0:T(8,128)(2,1)S(1)} async-done(((bf16[8,128,128]{1,2,0:T(8,128)(2,1)}), bf16[8,128,128]{1,2,0:T(8,128)(2,1)S(1)}, u32[]{:S(2)}, u32[]{:S(2)}) %all-to-all-start.2) | async-done | bytes 262176 | tf_op jit(solution)/shard_map/all_to_all | solution.py:37
  86.3 3.1 %fusion.x_all = bf16[128,1920]{1,0:T(8,128)(2,1)S(1)} fusion(bf16[128,1024]{0,1:T(8,128)(2,1)S(1)} %bitcast.145, bf16[1024,1920]{1,0:T(8,128)(2,1)} %param.14, bf16[1,128,1920]{2,1,0:T(8,128)(2,1)} %param.13), kind=kOutput, calls=%fused_computation.2 | convolution fusion | flops 504053760 | bytes 5177344 | tf_op jit(solution)/shard_map/dot_general | solution.py:556
  91.1 3.8 %collective-permute-start.3 = (bf16[128,1920]{1,0:T(8,128)(2,1)S(1)}, bf16[128,1920]{1,0:T(8,128)(2,1)}, u32[]{:S(2)}, u32[]{:S(2)}) collective-permute-start(bf16[128,1920]{1,0:T(8,128)(2,1)S(1)} %fusion.10.own), channel_id=1, source_target_pairs={{0,1},{1,2},{2,3},{3,4},{4,5},{5,6},{6,7},{7,8},{8,9},{9,10},{10,1... | collective-permute-start | bytes 1474568 | tf_op jit(solution)/shard_map/ppermute | solution.py:29
  96.8 5.4 %collective-permute-start.2 = (bf16[16,1920]{1,0:T(8,128)(2,1)}, bf16[16,1920]{1,0:T(8,128)(2,1)S(1)}, u32[]{:S(2)}, u32[]{:S(2)}) collective-permute-start(bf16[16,1920]{1,0:T(8,128)(2,1)} %get-tuple-element.66), channel_id=1, source_target_pairs={{0,2},{1,3},{2,4},{3,5},{4,6},{5,7},{6,8},{7,9},{8,10},{9,11},{10,... | collective-permute-start | bytes 184328 | tf_op jit(solution)/shard_map/ppermute | solution.py:29
  102.3 1.7 broadcast_select_fusion.1
  104.4 5.2 %collective-permute-done.5.following_far = bf16[16,1920]{1,0:T(8,128)(2,1)S(1)} collective-permute-done((bf16[16,1920]{1,0:T(8,128)(2,1)}, bf16[16,1920]{1,0:T(8,128)(2,1)S(1)}, u32[]{:S(2)}, u32[]{:S(2)}) %collective-permute-start.5) | collective-permute-done | bytes 61472 | tf_op jit(solution)/shard_map/ppermute | solution.py:29
  112.0 14.9 %shard_map.179 = (bf16[128,1920]{1,0:T(8,128)(2,1)}, bf16[128,1920]{1,0:T(8,128)(2,1)}, f32[16,24,128]{2,1,0:T(8,128)S(1)}) custom-call(bf16[16,1920]{1,0:T(8,128)(2,1)S(1)} %collective-permute-done.2.prev_far, bf16[128,1920]{1,0:T(8,128)(2,1)} %collective-permute-done.3.prev, bf16[128,1920]{1,0:T(8,128)(2,1)S(1)} %fusion.10.own, ...), custom_call_target="tpu_custom_call" | custom-call | flops 503316480 | bytes 12582912 | tf_op jit(solution)/shard_map/pallas_call | solution.py:232
  126.9 2.4 fusion.5
  130.2 8.9 %all-to-all-start.3 = ((bf16[8,176,128]{2,1,0:T(8,128)(2,1)}), bf16[8,176,128]{2,1,0:T(8,128)(2,1)}, u32[]{:S(2)}, u32[]{:S(2)}) async-start(bf16[8,176,128]{2,1,0:T(8,128)(2,1)} %pad_maximum_fusion.3), calls=%async_computation.3 | async-start | bytes 720896 | tf_op jit(solution)/shard_map/all_to_all | solution.py:37
  140.4 2.0 fusion.3
  142.4 2.1 fusion.2
  144.5 2.0 fusion.1
  146.5 8.7 %all-to-all-done.3 = bf16[8,176,128]{2,1,0:T(8,128)(2,1)} async-done(((bf16[8,176,128]{2,1,0:T(8,128)(2,1)}), bf16[8,176,128]{2,1,0:T(8,128)(2,1)}, u32[]{:S(2)}, u32[]{:S(2)}) %all-to-all-start.3) | async-done | bytes 360480 | tf_op jit(solution)/shard_map/all_to_all | solution.py:37
  156.3 7.9 %shard_map.180 = (bf16[1024,128]{1,0:T(8,128)(2,1)S(1)}, bf16[2,2,512,256]{3,2,1,0:T(8,128)(2,1)S(1)}, bf16[2,2,512,256]{3,2,1,0:T(8,128)(2,1)}) custom-call(s32[2]{0:T(128)S(1)} %pad_add_fusion.place, bf16[1024,128]{1,0:T(8,128)(2,1)S(1)} %bitcast.138, bf16[4096,256]{1,0:T(8,128)(2,1)S(1)} %bitcast.136, bf16[1024,128]{1,0:T(8,128)(2,1)S(1)} %copy-done.9, ...), custom_call_target="tpu_custom_call" | custom-call | flops 4000000000 | bytes 6000000 | tf_op jit(solution)/shard_map/pallas_call | solution.py:447
  167.6 4.6 %all-to-all-start.4 = ((bf16[4,1968,128]{2,1,0:T(8,128)(2,1)}), bf16[4,1968,128]{2,1,0:T(8,128)(2,1)}, u32[]{:S(2)}, u32[]{:S(2)}) async-start(bf16[4,1968,128]{2,1,0:T(8,128)(2,1)} %pad_maximum_fusion), calls=%async_computation.4 | async-start | bytes 4030464 | tf_op jit(solution)/shard_map/all_to_all | solution.py:37
  174.0 1.4 convert_add_fusion
  176.3 4.1 %collective-permute-start.9 = (bf16[2,512,256]{2,1,0:T(8,128)(2,1)}, bf16[2,512,256]{2,1,0:T(8,128)(2,1)}, u32[]{:S(2)}, u32[]{:S(2)}) collective-permute-start(bf16[2,512,256]{2,1,0:T(8,128)(2,1)} %fusion.11), channel_id=1, source_target_pairs={{0,8},{8,0},{1,9},{9,1},{2,10},{10,2},{3,11},{11,3},{4,12},{12,4},... | collective-permute-start | bytes 1572872 | tf_op jit(solution)/shard_map/ppermute | solution.py:33
  180.4 18.3 %all-to-all-done.4 = bf16[4,1968,128]{2,1,0:T(8,128)(2,1)} async-done(((bf16[4,1968,128]{2,1,0:T(8,128)(2,1)}), bf16[4,1968,128]{2,1,0:T(8,128)(2,1)}, u32[]{:S(2)}, u32[]{:S(2)}) %all-to-all-start.4) | async-done | bytes 2015264 | tf_op jit(solution)/shard_map/all_to_all | solution.py:37
  198.7 2.0 convert_reduce_fusion
  200.9 2.0 collective-permute-start.12
  205.7 4.0 %collective-permute-start.15 = (f32[48,128]{1,0:T(8,128)S(1)}, f32[48,128]{1,0:T(8,128)S(1)}, u32[]{:S(2)}, u32[]{:S(2)}) collective-permute-start(f32[48,128]{1,0:T(8,128)S(1)} %add_add_fusion), channel_id=1, source_target_pairs={{0,8},{8,0},{1,9},{9,1},{2,10},{10,2},{3,11},{11,3},{4,12},{12,4},... | collective-permute-start | bytes 73736 | tf_op jit(solution)/shard_map/ppermute | solution.py:33
  209.8 1.9 collective-permute-start.17
  211.7 1.9 collective-permute-start.16
  215.6 3.8 %collective-permute-done.16 = bf16[16,60,128]{2,1,0:T(8,128)(2,1)S(1)} collective-permute-done((bf16[16,60,128]{2,1,0:T(8,128)(2,1)S(1)}, bf16[16,60,128]{2,1,0:T(8,128)(2,1)S(1)}, u32[]{:S(2)}, u32[]{:S(2)}) %collective-permute-start.16) | collective-permute-done | bytes 245792 | tf_op jit(solution)/shard_map/ppermute | solution.py:523
  219.8 6.1 %collective-permute-done.18 = bf16[2,4,60,128]{3,1,0,2:T(4,128)(2,1)S(1)} collective-permute-done((bf16[2,4,60,128]{3,1,0,2:T(4,128)(2,1)S(1)}, bf16[2,4,60,128]{3,1,0,2:T(4,128)(2,1)S(1)}, u32[]{:S(2)}, u32[]{:S(2)}) %collective-permute-start.18) | collective-permute-done | bytes 122912 | tf_op jit(solution)/shard_map/ppermute | solution.py:33
  226.0 27.4 %all_to_all.31 = bf16[8,492,128]{2,1,0:T(8,128)(2,1)S(1)} all-to-all(bf16[8,492,128]{2,1,0:T(8,128)(2,1)S(1)} %copy_dynamic-update-slice_fusion), channel_id=1, replica_groups=mesh['zl'=2,'y'=4,'xa'=2,'xb'=2,'zh'=4,'c'=2] {'xa','zh'}, dimensions={0} | all-to-all | bytes 2015232 | tf_op jit(solution)/shard_map/all_to_all | solution.py:37
  (149 shorter events, 40.3 us)
Async XLA Ops:
  2.9 41.9 %copy-start.20 = (bf16[1,128,1024]{2,1,0:T(8,128)(2,1)S(1)}, bf16[1,128,1024]{2,1,0:T(8,128)(2,1)}, u32[]{:S(2)}) copy-start(bf16[1,128,1024]{2,1,0:T(8,128)(2,1)} %param.10) | copy-start | bytes 786436
  32.4 11.3 %collective-permute-start = (bf16[8,128,256]{1,2,0:T(8,128)(2,1)S(1)}, bf16[8,128,256]{1,2,0:T(8,128)(2,1)S(1)}, u32[]{:S(2)}, u32[]{:S(2)}) collective-permute-start(bf16[8,128,256]{1,2,0:T(8,128)(2,1)S(1)} %all_to_all.30), channel_id=1, source_target_pairs={{0,8},{8,0},{1,9},{9,1},{2,10},{10,2},{3,11},{11,3},{4,12},{12,4},... | collective-permute-start | bytes 1572872 | tf_op jit(solution)/shard_map/ppermute | solution.py:33
  44.8 5.1 %collective-permute-start.1 = (bf16[2,8,128,256]{2,3,1,0:T(8,128)(2,1)}, bf16[2,8,128,256]{2,3,1,0:T(8,128)(2,1)S(1)}, u32[]{:S(2)}, u32[]{:S(2)}) collective-permute-start(bf16[2,8,128,256]{2,3,1,0:T(8,128)(2,1)} %pad_maximum_fusion.1), channel_id=1, source_target_pairs={{0,1},{1,0},{2,3},{3,2},{4,5},{5,4},{6,7},{7,6},{8,9},{9,8},{10,11... | collective-permute-start | bytes 3145736 | tf_op jit(solution)/shard_map/ppermute | solution.py:33
  45.6 17.1 %all-to-all-start = ((bf16[8,128,128]{2,1,0:T(8,128)(2,1)}), bf16[8,128,128]{2,1,0:T(8,128)(2,1)S(1)}, u32[]{:S(2)}, u32[]{:S(2)}) async-start(bf16[8,128,128]{2,1,0:T(8,128)(2,1)} %bitcast.132), calls=%async_computation | async-start | bytes 524288 | tf_op jit(solution)/shard_map/all_to_all | solution.py:37
  62.7 12.8 %copy-start.23 = (bf16[15,128]{1,0:T(8,128)(2,1)S(1)}, bf16[15,128]{1,0:T(8,128)(2,1)}, u32[]{:S(2)}) copy-start(bf16[15,128]{1,0:T(8,128)(2,1)} %param.17) | copy-start | bytes 11524
  62.7 13.0 %copy-start.24 = (f32[1920]{0:T(1024)S(1)}, f32[1920]{0:T(1024)}, u32[]{:S(2)}) copy-start(f32[1920]{0:T(1024)} %param.18) | copy-start | bytes 23044
  62.7 13.0 %copy-start.22 = (f32[1920]{0:T(1024)S(1)}, f32[1920]{0:T(1024)}, u32[]{:S(2)}) copy-start(f32[1920]{0:T(1024)} %param.15) | copy-start | bytes 23044
  62.7 13.0 %copy-start.21 = (f32[3,7,1920]{2,1,0:T(8,128)S(1)}, f32[3,7,1920]{2,1,0:T(8,128)}, u32[]{:S(2)}) copy-start(f32[3,7,1920]{2,1,0:T(8,128)} %param.16) | copy-start | bytes 483844
  67.7 18.6 %copy-start.8 = (bf16[1024,128]{1,0:T(8,128)(2,1)}, bf16[1024,128]{1,0:T(8,128)(2,1)S(1)}, u32[]{:S(2)}) copy-start(bf16[1024,128]{1,0:T(8,128)(2,1)S(1)} %get-tuple-element.20.out) | copy-start | bytes 786436
  68.6 17.7 %all-to-all-start.2 = ((bf16[8,128,128]{1,2,0:T(8,128)(2,1)}), bf16[8,128,128]{1,2,0:T(8,128)(2,1)S(1)}, u32[]{:S(2)}, u32[]{:S(2)}) async-start(bf16[8,128,128]{1,2,0:T(8,128)(2,1)} %copy.116), calls=%async_computation.2 | async-start | bytes 524288 | tf_op jit(solution)/shard_map/all_to_all | solution.py:37
  72.9 24.0 %collective-permute-start.7 = (bf16[16,1920]{1,0:T(8,128)(2,1)S(1)}, bf16[16,1920]{1,0:T(8,128)(2,1)S(1)}, u32[]{:S(2)}, u32[]{:S(2)}) collective-permute-start(bf16[16,1920]{1,0:T(8,128)(2,1)S(1)} %slice_bitcast_fusion.1), channel_id=1, source_target_pairs={{2,0},{3,1},{4,2},{5,3},{6,4},{7,5},{8,6},{9,7},{10,8},{11,9},{12,... | collective-permute-start | bytes 184328 | tf_op jit(solution)/shard_map/ppermute | solution.py:29
  74.2 29.9 %collective-permute-start.6 = (bf16[128,1920]{1,0:T(8,128)(2,1)}, bf16[128,1920]{1,0:T(8,128)(2,1)}, u32[]{:S(2)}, u32[]{:S(2)}) collective-permute-start(bf16[128,1920]{1,0:T(8,128)(2,1)} %bitcast.19.cot_all), channel_id=1, source_target_pairs={{1,0},{2,1},{3,2},{4,3},{5,4},{6,5},{7,6},{8,7},{9,8},{10,9},{11,1... | collective-permute-start | bytes 1474568 | tf_op jit(solution)/shard_map/ppermute | solution.py:29
  89.8 19.8 %collective-permute-start.4 = (bf16[128,1920]{1,0:T(8,128)(2,1)S(1)}, bf16[128,1920]{1,0:T(8,128)(2,1)}, u32[]{:S(2)}, u32[]{:S(2)}) collective-permute-start(bf16[128,1920]{1,0:T(8,128)(2,1)S(1)} %fusion.10.own), channel_id=1, source_target_pairs={{1,0},{2,1},{3,2},{4,3},{5,4},{6,5},{7,6},{8,7},{9,8},{10,9},{11,1... | collective-permute-start | bytes 1474568 | tf_op jit(solution)/shard_map/ppermute | solution.py:29
  91.1 18.5 %collective-permute-start.3 = (bf16[128,1920]{1,0:T(8,128)(2,1)S(1)}, bf16[128,1920]{1,0:T(8,128)(2,1)}, u32[]{:S(2)}, u32[]{:S(2)}) collective-permute-start(bf16[128,1920]{1,0:T(8,128)(2,1)S(1)} %fusion.10.own), channel_id=1, source_target_pairs={{0,1},{1,2},{2,3},{3,4},{4,5},{5,6},{6,7},{7,8},{8,9},{9,10},{10,1... | collective-permute-start | bytes 1474568 | tf_op jit(solution)/shard_map/ppermute | solution.py:29
  95.5 14.0 %collective-permute-start.5 = (bf16[16,1920]{1,0:T(8,128)(2,1)}, bf16[16,1920]{1,0:T(8,128)(2,1)S(1)}, u32[]{:S(2)}, u32[]{:S(2)}) collective-permute-start(bf16[16,1920]{1,0:T(8,128)(2,1)} %get-tuple-element.65), channel_id=1, source_target_pairs={{2,0},{3,1},{4,2},{5,3},{6,4},{7,5},{8,6},{9,7},{10,8},{11,9},{12,... | collective-permute-start | bytes 184328 | tf_op jit(solution)/shard_map/ppermute | solution.py:29
  96.8 12.7 %collective-permute-start.2 = (bf16[16,1920]{1,0:T(8,128)(2,1)}, bf16[16,1920]{1,0:T(8,128)(2,1)S(1)}, u32[]{:S(2)}, u32[]{:S(2)}) collective-permute-start(bf16[16,1920]{1,0:T(8,128)(2,1)} %get-tuple-element.66), channel_id=1, source_target_pairs={{0,2},{1,3},{2,4},{3,5},{4,6},{5,7},{6,8},{7,9},{8,10},{9,11},{10,... | collective-permute-start | bytes 184328 | tf_op jit(solution)/shard_map/ppermute | solution.py:29
  104.1 35.1 %collective-permute-start.11 = (bf16[128,512]{0,1:T(8,128)(2,1)}, bf16[128,512]{0,1:T(8,128)(2,1)}, u32[]{:S(2)}, u32[]{:S(2)}) collective-permute-start(bf16[128,512]{0,1:T(8,128)(2,1)} %get-tuple-element.68), channel_id=1, source_target_pairs={{0,1},{1,0},{2,3},{3,2},{4,5},{5,4},{6,7},{7,6},{8,9},{9,8},{10,11... | collective-permute-start | bytes 393224 | tf_op jit(solution)/shard_map/ppermute | solution.py:33
  112.0 14.9 %copy-start.10 = (bf16[1024,1920]{1,0:T(8,128)(2,1)S(1)}, bf16[1024,1920]{1,0:T(8,128)(2,1)}, u32[]{:S(2)}) copy-start(bf16[1024,1920]{1,0:T(8,128)(2,1)} %param.14) | copy-start | bytes 11796484
  126.8 12.3 %collective-permute-start.10 = (bf16[128,1920]{1,0:T(8,128)(2,1)}, bf16[128,1920]{1,0:T(8,128)(2,1)S(1)}, u32[]{:S(2)}, u32[]{:S(2)}) collective-permute-start(bf16[128,1920]{1,0:T(8,128)(2,1)} %get-tuple-element.24), channel_id=1, source_target_pairs={{0,1},{1,0},{2,3},{3,2},{4,5},{5,4},{6,7},{7,6},{8,9},{9,8},{10,11... | collective-permute-start | bytes 1474568 | tf_op jit(solution)/shard_map/ppermute | solution.py:33
  130.2 25.1 %all-to-all-start.3 = ((bf16[8,176,128]{2,1,0:T(8,128)(2,1)}), bf16[8,176,128]{2,1,0:T(8,128)(2,1)}, u32[]{:S(2)}, u32[]{:S(2)}) async-start(bf16[8,176,128]{2,1,0:T(8,128)(2,1)} %pad_maximum_fusion.3), calls=%async_computation.3 | async-start | bytes 720896 | tf_op jit(solution)/shard_map/all_to_all | solution.py:37
  142.4 13.8 %copy-start.7 = (bf16[8,128,128]{2,1,0:T(8,128)(2,1)S(1)}, bf16[8,128,128]{2,1,0:T(8,128)(2,1)}, u32[]{:S(2)}) copy-start(bf16[8,128,128]{2,1,0:T(8,128)(2,1)} %copy-done.6) | copy-start | bytes 786436
  142.4 13.8 %copy-start.9 = (bf16[1024,128]{1,0:T(8,128)(2,1)S(1)}, bf16[1024,128]{1,0:T(8,128)(2,1)}, u32[]{:S(2)}) copy-start(bf16[1024,128]{1,0:T(8,128)(2,1)} %copy-done.8) | copy-start | bytes 786436
  165.3 7.8 %collective-permute-start.8 = (bf16[2,2,512,256]{3,2,1,0:T(8,128)(2,1)}, bf16[2,2,512,256]{3,2,1,0:T(8,128)(2,1)S(1)}, u32[]{:S(2)}, u32[]{:S(2)}) collective-permute-start(bf16[2,2,512,256]{3,2,1,0:T(8,128)(2,1)} %get-tuple-element.29), channel_id=1, source_target_pairs={{0,1},{1,0},{2,3},{3,2},{4,5},{5,4},{6,7},{7,6},{8,9},{9,8},{10,11... | collective-permute-start | bytes 3145736 | tf_op jit(solution)/shard_map/ppermute | solution.py:33
  167.6 31.0 %all-to-all-start.4 = ((bf16[4,1968,128]{2,1,0:T(8,128)(2,1)}), bf16[4,1968,128]{2,1,0:T(8,128)(2,1)}, u32[]{:S(2)}, u32[]{:S(2)}) async-start(bf16[4,1968,128]{2,1,0:T(8,128)(2,1)} %pad_maximum_fusion), calls=%async_computation.4 | async-start | bytes 4030464 | tf_op jit(solution)/shard_map/all_to_all | solution.py:37
  176.3 37.3 %collective-permute-start.9 = (bf16[2,512,256]{2,1,0:T(8,128)(2,1)}, bf16[2,512,256]{2,1,0:T(8,128)(2,1)}, u32[]{:S(2)}, u32[]{:S(2)}) collective-permute-start(bf16[2,512,256]{2,1,0:T(8,128)(2,1)} %fusion.11), channel_id=1, source_target_pairs={{0,8},{8,0},{1,9},{9,1},{2,10},{10,2},{3,11},{11,3},{4,12},{12,4},... | collective-permute-start | bytes 1572872 | tf_op jit(solution)/shard_map/ppermute | solution.py:33
  200.7 2.5 collective-permute-start.13
  200.8 3.3 %collective-permute-start.14 = (f32[48,128]{1,0:T(8,128)S(1)}, f32[48,128]{1,0:T(8,128)S(1)}, u32[]{:S(2)}, u32[]{:S(2)}) collective-permute-start(f32[48,128]{1,0:T(8,128)S(1)} %slice.154), channel_id=1, source_target_pairs={{0,129},{1,128},{128,1},{129,0},{2,131},{3,130},{130,3},{131,2},{4... | collective-permute-start | bytes 73736 | tf_op jit(solution)/shard_map/ppermute | solution.py:514
  200.9 4.1 %collective-permute-start.12 = (f32[48,128]{1,0:T(8,128)S(1)}, f32[48,128]{1,0:T(8,128)S(1)}, u32[]{:S(2)}, u32[]{:S(2)}) collective-permute-start(f32[48,128]{1,0:T(8,128)S(1)} %slice.154), channel_id=1, source_target_pairs={{0,128},{1,129},{128,0},{129,1},{2,130},{3,131},{130,2},{131,3},{4... | collective-permute-start | bytes 73736 | tf_op jit(solution)/shard_map/ppermute | solution.py:514
  205.7 7.9 %collective-permute-start.15 = (f32[48,128]{1,0:T(8,128)S(1)}, f32[48,128]{1,0:T(8,128)S(1)}, u32[]{:S(2)}, u32[]{:S(2)}) collective-permute-start(f32[48,128]{1,0:T(8,128)S(1)} %add_add_fusion), channel_id=1, source_target_pairs={{0,8},{8,0},{1,9},{9,1},{2,10},{10,2},{3,11},{11,3},{4,12},{12,4},... | collective-permute-start | bytes 73736 | tf_op jit(solution)/shard_map/ppermute | solution.py:33
  209.8 5.7 %collective-permute-start.17 = (bf16[16,60,128]{2,1,0:T(8,128)(2,1)S(1)}, bf16[16,60,128]{2,1,0:T(8,128)(2,1)S(1)}, u32[]{:S(2)}, u32[]{:S(2)}) collective-permute-start(bf16[16,60,128]{2,1,0:T(8,128)(2,1)S(1)} %fusion.12), channel_id=1, source_target_pairs={{0,1},{1,129},{128,0},{129,128},{2,3},{3,131},{130,2},{131,130},{4... | collective-permute-start | bytes 737288 | tf_op jit(solution)/shard_map/ppermute | solution.py:523
  211.7 7.7 %collective-permute-start.16 = (bf16[16,60,128]{2,1,0:T(8,128)(2,1)S(1)}, bf16[16,60,128]{2,1,0:T(8,128)(2,1)S(1)}, u32[]{:S(2)}, u32[]{:S(2)}) collective-permute-start(bf16[16,60,128]{2,1,0:T(8,128)(2,1)S(1)} %fusion.13), channel_id=1, source_target_pairs={{0,0},{1,128},{128,1},{129,129},{2,2},{3,130},{130,3},{131,131},{4... | collective-permute-start | bytes 737288 | tf_op jit(solution)/shard_map/ppermute | solution.py:523
  219.7 6.2 %collective-permute-start.18 = (bf16[2,4,60,128]{3,1,0,2:T(4,128)(2,1)S(1)}, bf16[2,4,60,128]{3,1,0,2:T(4,128)(2,1)S(1)}, u32[]{:S(2)}, u32[]{:S(2)}) collective-permute-start(bf16[2,4,60,128]{3,1,0,2:T(4,128)(2,1)S(1)} %fusion.15), channel_id=1, source_target_pairs={{0,8},{8,0},{1,9},{9,1},{2,10},{10,2},{3,11},{11,3},{4,12},{12,4},... | collective-permute-start | bytes 368648 | tf_op jit(solution)/shard_map/ppermute | solution.py:33
  (16 other events, 84.2 us)
where the time goes:
time: 261 us; the launch traced here: 259 us
  waiting for transfers between devices  75.1 us (29%)
  blocking collectives  56.8 us (22%)
  starting transfers between devices  50.2 us (19%)
  Pallas kernels  28.4 us (11%)
  local copies, waits for them, and re-layouts  21.6 us (8%)
  other arithmetic  13 us (5%)
  matrix products  12.8 us (5%)
    all_to_all x2, blocking collectives, exchange(): return lax.all_to_all(x, axes, split_axis=0, concat_axis=0, tiled=True)  56.8 us
    all_to_all x4, waiting for transfers between devices, exchange(): return lax.all_to_all(x, axes, split_axis=0, concat_axis=0, tiled=True)  46.9 us
    all_to_all x4, starting transfers between devices, exchange(): return lax.all_to_all(x, axes, split_axis=0, concat_axis=0, tiled=True)  20.6 us
    ppermute x8, waiting for transfers between devices, swap(): return lax.ppermute(x, axis, [(0, 1), (1, 0)])  16.7 us
    pallas_call x1, Pallas kernels, hyena(): pl.pallas_call(hyena_kernel, grid=(FILTERS,), in_specs=[part(FAR), part(r...  14.9 us
    ppermute x6, starting transfers between devices, from_behind(): return lax.ppermute(x, CTX_AXES, pairs)  14.4 us
    unnamed x65, local copies, waits for them, and re-layouts  13.3 us
    ppermute x8, starting transfers between devices, swap(): return lax.ppermute(x, axis, [(0, 1), (1, 0)])  9.21 us
  transfers between devices with their start and end apart: 23, of which 11 were waited for; matrix products, arithmetic and copies ran while one was open for 11% of the time, Pallas kernels for 6%

commit v1 on v0

--- a/solution.py
+++ b/solution.py
@@ -468,23 +468,14 @@
 
 
 def gather_keys(kv_own):
-    rows = kv_own.shape[1]
     wide = jnp.stack([kv_own, swap(kv_own, "xb")])
     both = jnp.stack([wide, swap(wide, "c")])
-    both = both.reshape(2, 2, 2, 4, rows, 2 * HDIM).transpose(2, 0, 1, 3, 4, 5)
-    return both.reshape(32 * rows, 2 * HDIM)
-
-
-def scatter_keys(same_core, other_core):
-    f32 = jnp.float32
-    parts = same_core.astype(f32) + swap(other_core, "c").astype(f32)
-    parts = parts[:, 0] + swap(parts[:, 1].astype(jnp.bfloat16), "xb").astype(f32)
-    return parts.reshape(8, -1, 2 * HDIM).astype(jnp.bfloat16)
-
-
-def weight_sum(attention, grad_residual, small_part):
+    both = both.reshape(2, 2, 2, 4, 2, -1, HDIM).transpose(2, 0, 1, 3, 5, 4, 6)
+    return both.reshape(-1, 2 * HDIM)
+
+
+def weight_pieces(attention, grad_residual):
     core = lax.axis_index("c")
-    zl = lax.axis_index("zl")
     half = AD // 2
     mine = jnp.where(core == 0, attention[:, :half], attention[:, half:])
     theirs = jnp.where(core == 0, attention[:, half:], attention[:, :half])
@@ -492,42 +483,45 @@
     rows_g = jnp.concatenate([grad_residual, swap(grad_residual, "c")], axis=0)
     peers = lax.axis_size("y")
     width = half // peers
-    pieces = jnp.stack(
-        [
-            lax.dot_general(
-                rows_g,
-                rows_a[:, i * width : (i + 1) * width],
-                (((0,), (0,)), ((), ())),
-                preferred_element_type=jnp.float32,
-            ).astype(jnp.bfloat16)
-            for i in range(peers)
-        ]
-    )
-    small_rows = small_part.reshape(1, -1, width).astype(jnp.bfloat16)
-    small_rows = jnp.broadcast_to(small_rows, (peers,) + small_rows.shape[1:])
-    total = exchange(jnp.concatenate([pieces, small_rows], axis=1), "y")
-    total = jnp.sum(total.astype(jnp.float32), axis=0)
-    small_part = total[D:]
-    total = total[:D].astype(jnp.bfloat16).reshape(16, 2, D // 32, width)
-
-    def flip(x, by):
-        return lax.ppermute(x, ("zl", "c"), [(i, i ^ by) for i in range(4)])
-
-    small_part = (small_part + flip(small_part, 2)) + (flip(small_part, 1) + flip(small_part, 3))
-    small_part = small_part + swap(small_part, "xb")
+    at = lax.axis_index("y")
+    pieces = []
+    for step in range(peers):
+        columns = lax.dynamic_slice_in_dim(rows_a, (at + step) % peers * width, width, axis=1)
+        piece = lax.dot_general(
+            rows_g, columns, (((0,), (0,)), ((), ())), preferred_element_type=jnp.float32
+        )
+        pieces.append(piece.astype(jnp.bfloat16))
+    return lax.optimization_barrier(pieces)
+
+
+def weight_over_y(pieces):
+    peers = len(pieces)
+    total = pieces[0].astype(jnp.float32)
+    for step in range(1, peers):
+        pairs = [(i, (i + step) % peers) for i in range(peers)]
+        total = total + lax.ppermute(pieces[step], "y", pairs).astype(jnp.float32)
+    return total.astype(jnp.bfloat16)
+
+
+def weight_over_zl(total):
+    zl = lax.axis_index("zl")
+    total = total.reshape(16, 2, D // 32, -1)
     halves = (total[:, 0], total[:, 1])
     received = []
     for turn in range(2):
         piece = jnp.where(zl == 0, halves[turn], halves[1 - turn])
         pairs = [(a * 2 + b, b * 2 + (a ^ turn)) for a in range(2) for b in range(2)]
         received.append(lax.ppermute(piece, ("zl", "c"), pairs).astype(jnp.float32))
-    total = (received[0] + received[1]).astype(jnp.bfloat16)
+    return (received[0] + received[1]).astype(jnp.bfloat16)
+
+
+def weight_over_xb(total):
     xb = lax.axis_index("xb")
-    total = total.reshape(2, 2, 4, D // 32, width)
+    total = total.reshape(2, 2, 4, D // 32, -1)
     mine = jnp.where(xb == 0, total[:, 0], total[:, 1]).astype(jnp.float32)
     theirs = jnp.where(xb == 0, total[:, 1], total[:, 0])
     total = mine + swap(theirs, "xb").astype(jnp.float32)
-    return total.astype(jnp.bfloat16).reshape(8, D // 32, width), small_part
+    return total.astype(jnp.bfloat16).reshape(8, D // 32, -1)
 
 
 def local(
@@ -545,10 +539,12 @@
     tok_rows = query_in.shape[1]
     matrices = toeplitz(filters)
     cot_sides = (from_behind(cotangent[0], -1), from_behind(cotangent[0, :FAR], -2))
-    kv_send = jnp.concatenate([to_heads(key_in[0]), to_heads(value_in[0])], axis=2)
-    kv_own = exchange(kv_send, HEAD_AXES)
-    query_rows = exchange(to_heads(query_in[0]), HEAD_AXES).reshape(8 * tok_rows, HDIM)
-    kv_all = gather_keys(kv_own)
+    qkv_send = jnp.concatenate(
+        [to_heads(query_in[0]), to_heads(key_in[0]), to_heads(value_in[0])], axis=1
+    )
+    qkv_own = exchange(qkv_send, HEAD_AXES)
+    query_rows = qkv_own[:, :tok_rows].reshape(8 * tok_rows, HDIM)
+    kv_all = gather_keys(qkv_own[:, tok_rows:])
     query_total = 8 * tok_rows
     place = jnp.stack([lax.axis_index("xb"), lax.axis_index("c")]).astype(jnp.int32)
     head_out, log_total = attend(place, query_rows, kv_all)
@@ -587,24 +583,34 @@
     grad_recv = exchange(
         jnp.concatenate([to_heads(grad_attention), small_send], axis=1), HEAD_AXES
     )
+    weight_part = weight_over_y(weight_pieces(attention, grad_residual))
     grad_rows_all = grad_recv[:, :tok_rows].reshape(query_total, HDIM)
     small_part = jnp.sum(grad_recv[:, tok_rows:].astype(jnp.float32), axis=0)
-    weight_part, small_part = weight_sum(attention, grad_residual, small_part)
-    small_high = small_part.reshape(-1, HDIM).astype(jnp.bfloat16)
+    sequences = lax.axis_size(DP_AXES)
+    small_part = exchange(
+        jnp.broadcast_to(small_part[None], (sequences,) + small_part.shape), DP_AXES
+    )
+    small_part = jnp.sum(small_part, axis=0)
+    small_part = small_part + swap(small_part, "c")
+    small_part = small_part + swap(small_part, "xb")
+    small_part = small_part.astype(jnp.bfloat16)
 
     grad_query, same_core, other_core = attend_back(
         place, query_rows, kv_all, head_out, log_total, grad_rows_all
     )
     dq_send = grad_query.reshape(8, tok_rows, HDIM)
-    dkv = scatter_keys(same_core, other_core)
-    dp_rows = weight_part.shape[2] // HDIM
-    weight_rows = weight_part.shape[1] * dp_rows
+    dkv = same_core.astype(jnp.float32) + swap(other_core, "c").astype(jnp.float32)
+    weight_part = weight_over_zl(weight_part)
+    dkv = dkv[:, 0] + swap(dkv[:, 1].astype(jnp.bfloat16), "xb").astype(jnp.float32)
+    dkv = dkv.reshape(8, tok_rows, 2 * HDIM).astype(jnp.bfloat16)
+    weight_part = weight_over_xb(weight_part)
+    weight_rows = weight_part.size // (8 * HDIM)
     last_send = jnp.concatenate(
         [
             dq_send,
             dkv[:, :, :HDIM],
             dkv[:, :, HDIM:],
-            jnp.broadcast_to(small_high[None], (8,) + small_high.shape),
+            jnp.broadcast_to(small_part[None], (8,) + small_part.shape),
             weight_part.reshape(8, weight_rows, HDIM),
         ],
         axis=1,
@@ -613,12 +619,12 @@
     grad_query = from_heads(last[:, :tok_rows])
     grad_key = from_heads(last[:, tok_rows : 2 * tok_rows])
     grad_value = from_heads(last[:, 2 * tok_rows : 3 * tok_rows])
-    at = 3 * tok_rows
-    small_back = last[:, at : at + small_rows].astype(jnp.float32)
+    sums_back = last[:, 3 * tok_rows :].astype(jnp.float32)
+    small_back = sums_back[:, :small_rows]
     small_back = small_back.reshape(FILTERS + 1, SMALL, FCH)[:FILTERS].transpose(1, 0, 2)
     grad_filters = small_back[SMALL - 1]
     small_back = small_back.reshape(SMALL, D)
-    grad_weight = jnp.sum(last[:, at + small_rows :].astype(jnp.float32), axis=0)
+    grad_weight = jnp.sum(sums_back[:, small_rows:], axis=0)
     grad_weight = grad_weight.reshape(D // 32, -1).T
     return (
         layer_out[None],

time: 261 us -> 256 us (0.981)
  waiting for transfers between devices: 75.1 us -> 55.9 us
  blocking collectives: 56.8 us -> 72.6 us
  starting transfers between devices: 50.2 us -> 45.3 us
  local copies, waits for them, and re-layouts: 21.6 us -> 26.3 us
  other arithmetic: 13 us -> 10.3 us
    all_to_all x4 -> x3, waiting for transfers between devices: 46.9 us -> 8.39 us  [exchange(): return lax.all_to_all(x, axes, split_axis=0, concat_axis=0, tiled=True)]
    all_to_all x2, blocking collectives: 56.8 us -> 72.6 us  [exchange(): return lax.all_to_all(x, axes, split_axis=0, concat_axis=0, tiled=True)]
    ppermute x8 -> x9, waiting for transfers between devices: 16.7 us -> 26.5 us  [swap(): return lax.ppermute(x, axis, [(0, 1), (1, 0)])]
    ppermute x8 -> x9, starting transfers between devices: 9.21 us -> 3.63 us  [swap(): return lax.ppermute(x, axis, [(0, 1), (1, 0)])]
    ppermute x5, waiting for transfers between devices: 6.26 us -> 11.5 us  [the longest x3 7.06 us: weight_over_y(): total = total + lax.ppermute(pieces[step], 'y', pairs).astype(jnp.float32)]
    ppermute x6, waiting for transfers between devices: 5.18 us -> 9.6 us  [from_behind(): return lax.ppermute(x, CTX_AXES, pairs)]
    ppermute x6, starting transfers between devices: 14.4 us -> 11.3 us  [from_behind(): return lax.ppermute(x, CTX_AXES, pairs)]
    all_to_all x4 -> x3, starting transfers between devices: 20.6 us -> 22.5 us  [exchange(): return lax.all_to_all(x, axes, split_axis=0, concat_axis=0, tiled=True)]
  transfers between devices with their start and end apart: 23 -> 23, of which waited for: 11 -> 9; matrix products, arithmetic and copies ran while one was open for 11% -> 14% of each run, Pallas kernels for 6% -> 11%
where the time goes in v1:
time: 256 us; the launch traced here: 254 us
  blocking collectives  72.6 us (28%)
  waiting for transfers between devices  55.9 us (22%)
  starting transfers between devices  45.3 us (18%)
  Pallas kernels  28.4 us (11%)
  local copies, waits for them, and re-layouts  26.3 us (10%)
  matrix products  13.7 us (5%)
  other arithmetic  10.3 us (4%)
    all_to_all x2, blocking collectives, exchange(): return lax.all_to_all(x, axes, split_axis=0, concat_axis=0, tiled=True)  72.6 us
    ppermute x9, waiting for transfers between devices, swap(): return lax.ppermute(x, axis, [(0, 1), (1, 0)])  26.5 us
    all_to_all x3, starting transfers between devices, exchange(): return lax.all_to_all(x, axes, split_axis=0, concat_axis=0, tiled=True)  22.5 us
    pallas_call x1, Pallas kernels, hyena(): pl.pallas_call(hyena_kernel, grid=(FILTERS,), in_specs=[part(FAR), part(r...  14.9 us
    unnamed x56, local copies, waits for them, and re-layouts  13 us
    ppermute x6, starting transfers between devices, from_behind(): return lax.ppermute(x, CTX_AXES, pairs)  11.3 us
    ppermute x6, waiting for transfers between devices, from_behind(): return lax.ppermute(x, CTX_AXES, pairs)  9.6 us
    all_to_all x3, waiting for transfers between devices, exchange(): return lax.all_to_all(x, axes, split_axis=0, concat_axis=0, tiled=True)  8.39 us
  transfers between devices with their start and end apart: 23, of which 9 were waited for; matrix products, arithmetic and copies ran while one was open for 14% of the time, Pallas kernels for 11%

profile of v1, /device:TPU:32, one launch (start us, length us, event | category | flops | bytes accessed | tf_op | source)
XLA Modules:
  0.0 253.8 jit_solution(13425830518810762768)
XLA Ops:
  4.1 34.9 %all_to_all.25 = bf16[8,384,128]{1,2,0:T(8,128)(2,1)S(1)} all-to-all(bf16[8,384,128]{1,2,0:T(8,128)(2,1)S(1)} %pad_maximum_fusion.1), channel_id=1, replica_groups=mesh['zl'=2,'y'=4,'xa'=2,'xb'=2,'zh'=4,'c'=2] {'xa','zh'}, dimensions={0} | all-to-all | bytes 1572864 | tf_op jit(solution)/shard_map/all_to_all | solution.py:37
  39.8 10.9 %collective-permute-done = bf16[8,256,128]{1,2,0:T(8,128)(2,1)S(1)} collective-permute-done((bf16[8,256,128]{1,2,0:T(8,128)(2,1)S(1)}, bf16[8,256,128]{1,2,0:T(8,128)(2,1)S(1)}, u32[]{:S(2)}, u32[]{:S(2)}) %collective-permute-start) | collective-permute-done | bytes 524320 | tf_op jit(solution)/shard_map/ppermute | solution.py:33
  54.5 1.6 copy.112
  57.6 2.2 copy.113
  60.1 5.0 %shard_map.177 = (bf16[1024,128]{1,0:T(8,128)(2,1)S(1)}, f32[1,1024]{1,0:T(1,128)S(1)}) custom-call(s32[2]{0:T(128)S(1)} %pad_add_fusion.place, bf16[1024,128]{1,0:T(8,128)(2,1)S(1)} %bitcast.131, bf16[4096,256]{1,0:T(8,128)(2,1)S(1)} %bitcast.129), custom_call_target="tpu_custom_call" | custom-call | flops 1600000000 | bytes 3000000 | tf_op jit(solution)/shard_map/pallas_call | solution.py:362
  66.0 5.9 %all-to-all-start.1 = ((bf16[8,128,128]{1,2,0:T(8,128)(2,1)}), bf16[8,128,128]{1,2,0:T(8,128)(2,1)S(1)}, u32[]{:S(2)}, u32[]{:S(2)}) async-start(bf16[8,128,128]{1,2,0:T(8,128)(2,1)} %copy.114), calls=%async_computation.1 | async-start | bytes 524288 | tf_op jit(solution)/shard_map/all_to_all | solution.py:37
  72.7 1.5 collective-permute-start.7
  77.1 8.4 %all-to-all-done.1 = bf16[8,128,128]{1,2,0:T(8,128)(2,1)S(1)} async-done(((bf16[8,128,128]{1,2,0:T(8,128)(2,1)}), bf16[8,128,128]{1,2,0:T(8,128)(2,1)S(1)}, u32[]{:S(2)}, u32[]{:S(2)}) %all-to-all-start.1) | async-done | bytes 262176 | tf_op jit(solution)/shard_map/all_to_all | solution.py:37
  85.5 3.1 %fusion.x_all = bf16[128,1920]{1,0:T(8,128)(2,1)S(1)} fusion(bf16[128,1024]{0,1:T(8,128)(2,1)S(1)} %bitcast.138, bf16[1024,1920]{1,0:T(8,128)(2,1)} %param.14, bf16[1,128,1920]{2,1,0:T(8,128)(2,1)} %param.13), kind=kOutput, calls=%fused_computation.1 | convolution fusion | flops 504053760 | bytes 5177344 | tf_op jit(solution)/shard_map/dot_general | solution.py:552
  89.0 2.1 collective-permute-start.3
  93.0 3.9 %collective-permute-start.2 = (bf16[16,1920]{1,0:T(8,128)(2,1)}, bf16[16,1920]{1,0:T(8,128)(2,1)S(1)}, u32[]{:S(2)}, u32[]{:S(2)}) collective-permute-start(bf16[16,1920]{1,0:T(8,128)(2,1)} %get-tuple-element.76), channel_id=1, source_target_pairs={{0,2},{1,3},{2,4},{3,5},{4,6},{5,7},{6,8},{7,9},{8,10},{9,11},{10,... | collective-permute-start | bytes 184328 | tf_op jit(solution)/shard_map/ppermute | solution.py:29
  98.2 1.7 broadcast_select_fusion
  101.2 8.5 %collective-permute-done.5.following_far = bf16[16,1920]{1,0:T(8,128)(2,1)S(1)} collective-permute-done((bf16[16,1920]{1,0:T(8,128)(2,1)}, bf16[16,1920]{1,0:T(8,128)(2,1)S(1)}, u32[]{:S(2)}, u32[]{:S(2)}) %collective-permute-start.5) | collective-permute-done | bytes 61472 | tf_op jit(solution)/shard_map/ppermute | solution.py:29
  112.1 14.9 %shard_map.179 = (bf16[128,1920]{1,0:T(8,128)(2,1)}, bf16[128,1920]{1,0:T(8,128)(2,1)}, f32[16,24,128]{2,1,0:T(8,128)S(1)}) custom-call(bf16[16,1920]{1,0:T(8,128)(2,1)S(1)} %collective-permute-done.2.prev_far, bf16[128,1920]{1,0:T(8,128)(2,1)} %collective-permute-done.3.prev, bf16[128,1920]{1,0:T(8,128)(2,1)S(1)} %fusion.6.own, ...), custom_call_target="tpu_custom_call" | custom-call | flops 503316480 | bytes 12582912 | tf_op jit(solution)/shard_map/pallas_call | solution.py:232
  127.0 2.4 fusion.1
  130.3 12.0 %all-to-all-start.2 = ((bf16[8,176,128]{2,1,0:T(8,128)(2,1)}), bf16[8,176,128]{2,1,0:T(8,128)(2,1)S(1)}, u32[]{:S(2)}, u32[]{:S(2)}) async-start(bf16[8,176,128]{2,1,0:T(8,128)(2,1)} %pad_maximum_fusion.2), calls=%async_computation.2 | async-start | bytes 720896 | tf_op jit(solution)/shard_map/all_to_all | solution.py:37
  143.5 2.0 convolution_convert_fusion
  145.5 2.0 convolution_convert_fusion.1
  147.5 2.1 convolution_convert_fusion.2
  149.6 2.0 convolution_convert_fusion.3
  151.6 1.6 collective-permute-start.14
  153.2 2.9 %collective-permute-start.15 = (bf16[1920,128]{1,0:T(8,128)(2,1)}, bf16[1920,128]{1,0:T(8,128)(2,1)}, u32[]{:S(2)}, u32[]{:S(2)}) collective-permute-start(bf16[1920,128]{1,0:T(8,128)(2,1)} %convolution_convert_fusion.1), channel_id=1, source_target_pairs={{0,64},{32,96},{64,0},{96,32},{1,65},{33,97},{65,1},{97,33},{2,66}... | collective-permute-start | bytes 1474568 | tf_op jit(solution)/shard_map/ppermute | solution.py:502
  158.3 4.7 %all-to-all-start.3 = ((f32[8,48,128]{2,1,0:T(8,128)}), f32[8,48,128]{2,1,0:T(8,128)}, u32[]{:S(2)}, u32[]{:S(2)}) async-start(f32[8,48,128]{2,1,0:T(8,128)} %broadcast_in_dim.26), calls=%async_computation.3 | async-start | bytes 393216 | tf_op jit(solution)/shard_map/all_to_all | solution.py:37
  164.0 7.9 %shard_map.180 = (bf16[1024,128]{1,0:T(8,128)(2,1)S(1)}, bf16[2,2,512,256]{3,2,1,0:T(8,128)(2,1)S(1)}, bf16[2,2,512,256]{3,2,1,0:T(8,128)(2,1)}) custom-call(s32[2]{0:T(128)S(1)} %pad_add_fusion.place, bf16[1024,128]{1,0:T(8,128)(2,1)S(1)} %bitcast.132, bf16[4096,256]{1,0:T(8,128)(2,1)S(1)} %bitcast.130, bf16[1024,128]{1,0:T(8,128)(2,1)S(1)} %copy-done.9, ...), custom_call_target="tpu_custom_call" | custom-call | flops 4000000000 | bytes 6000000 | tf_op jit(solution)/shard_map/pallas_call | solution.py:447
  172.8 7.1 %collective-permute-done.15 = bf16[1920,128]{1,0:T(8,128)(2,1)} collective-permute-done((bf16[1920,128]{1,0:T(8,128)(2,1)}, bf16[1920,128]{1,0:T(8,128)(2,1)}, u32[]{:S(2)}, u32[]{:S(2)}) %collective-permute-start.15) | collective-permute-done | bytes 491552 | tf_op jit(solution)/shard_map/ppermute | solution.py:502
  179.9 1.6 add_convert_fusion
  182.3 1.9 collective-permute-start.17
  186.8 3.5 %collective-permute-done.17 = bf16[16,60,128]{2,1,0:T(8,128)(2,1)S(1)} collective-permute-done((bf16[16,60,128]{2,1,0:T(8,128)(2,1)}, bf16[16,60,128]{2,1,0:T(8,128)(2,1)S(1)}, u32[]{:S(2)}, u32[]{:S(2)}) %collective-permute-start.17) | collective-permute-done | bytes 245792 | tf_op jit(solution)/shard_map/ppermute | solution.py:514
  191.3 1.4 convert_add_fusion
  192.9 2.1 collective-permute-start.19
  195.0 14.8 %collective-permute-done.19 = bf16[2,4,60,128]{3,2,1,0:T(8,128)(2,1)S(1)} collective-permute-done((bf16[2,4,60,128]{3,2,1,0:T(8,128)(2,1)S(1)}, bf16[2,4,60,128]{3,2,1,0:T(8,128)(2,1)S(1)}, u32[]{:S(2)}, u32[]{:S(2)}) %collective-permute-start.19) | collective-permute-done | bytes 122912 | tf_op jit(solution)/shard_map/ppermute | solution.py:33
  210.2 37.7 %all_to_all.26 = bf16[8,492,128]{2,1,0:T(8,128)(2,1)S(1)} all-to-all(bf16[8,492,128]{2,1,0:T(8,128)(2,1)S(1)} %constant_dynamic-update-slice_fusion.2), channel_id=1, replica_groups=mesh['zl'=2,'y'=4,'xa'=2,'xb'=2,'zh'=4,'c'=2] {'xa','zh'}, dimensions={0} | all-to-all | bytes 2015232 | tf_op jit(solution)/shard_map/all_to_all | solution.py:37
  (139 shorter events, 38.4 us)
Async XLA Ops:
  39.1 11.6 %collective-permute-start = (bf16[8,256,128]{1,2,0:T(8,128)(2,1)S(1)}, bf16[8,256,128]{1,2,0:T(8,128)(2,1)S(1)}, u32[]{:S(2)}, u32[]{:S(2)}) collective-permute-start(bf16[8,256,128]{1,2,0:T(8,128)(2,1)S(1)} %get-tuple-element.74), channel_id=1, source_target_pairs={{0,8},{8,0},{1,9},{9,1},{2,10},{10,2},{3,11},{11,3},{4,12},{12,4},... | collective-permute-start | bytes 1572872 | tf_op jit(solution)/shard_map/ppermute | solution.py:33
  50.8 3.8 %collective-permute-start.1 = (bf16[2,8,256,128]{2,3,1,0:T(8,128)(2,1)S(1)}, bf16[2,8,256,128]{2,3,1,0:T(8,128)(2,1)}, u32[]{:S(2)}, u32[]{:S(2)}) collective-permute-start(bf16[2,8,256,128]{2,3,1,0:T(8,128)(2,1)S(1)} %pad_maximum_fusion), channel_id=1, source_target_pairs={{0,1},{1,0},{2,3},{3,2},{4,5},{5,4},{6,7},{7,6},{8,9},{9,8},{10,11... | collective-permute-start | bytes 3145736 | tf_op jit(solution)/shard_map/ppermute | solution.py:33
  50.9 49.1 %collective-permute-start.6 = (bf16[128,1920]{1,0:T(8,128)(2,1)}, bf16[128,1920]{1,0:T(8,128)(2,1)}, u32[]{:S(2)}, u32[]{:S(2)}) collective-permute-start(bf16[128,1920]{1,0:T(8,128)(2,1)} %bitcast.19.cot_all), channel_id=1, source_target_pairs={{1,0},{2,1},{3,2},{4,3},{5,4},{6,5},{7,6},{8,7},{9,8},{10,9},{11,1... | collective-permute-start | bytes 1474568 | tf_op jit(solution)/shard_map/ppermute | solution.py:29
  60.1 14.2 %copy-start.18 = (bf16[15,128]{1,0:T(8,128)(2,1)S(1)}, bf16[15,128]{1,0:T(8,128)(2,1)}, u32[]{:S(2)}) copy-start(bf16[15,128]{1,0:T(8,128)(2,1)} %param.17) | copy-start | bytes 11524
  60.1 14.4 %copy-start.16 = (f32[3,7,1920]{2,1,0:T(8,128)S(1)}, f32[3,7,1920]{2,1,0:T(8,128)}, u32[]{:S(2)}) copy-start(f32[3,7,1920]{2,1,0:T(8,128)} %param.16) | copy-start | bytes 483844
  60.1 14.4 %copy-start.17 = (f32[1920]{0:T(1024)S(1)}, f32[1920]{0:T(1024)}, u32[]{:S(2)}) copy-start(f32[1920]{0:T(1024)} %param.15) | copy-start | bytes 23044
  60.1 14.4 %copy-start.19 = (f32[1920]{0:T(1024)S(1)}, f32[1920]{0:T(1024)}, u32[]{:S(2)}) copy-start(f32[1920]{0:T(1024)} %param.18) | copy-start | bytes 23044
  65.1 20.4 %copy-start.8 = (bf16[1024,128]{1,0:T(8,128)(2,1)}, bf16[1024,128]{1,0:T(8,128)(2,1)S(1)}, u32[]{:S(2)}) copy-start(bf16[1024,128]{1,0:T(8,128)(2,1)S(1)} %get-tuple-element.24.out) | copy-start | bytes 786436
  66.0 19.5 %all-to-all-start.1 = ((bf16[8,128,128]{1,2,0:T(8,128)(2,1)}), bf16[8,128,128]{1,2,0:T(8,128)(2,1)S(1)}, u32[]{:S(2)}, u32[]{:S(2)}) async-start(bf16[8,128,128]{1,2,0:T(8,128)(2,1)} %copy.114), calls=%async_computation.1 | async-start | bytes 524288 | tf_op jit(solution)/shard_map/all_to_all | solution.py:37
  72.7 24.2 %collective-permute-start.7 = (bf16[16,1920]{1,0:T(8,128)(2,1)S(1)}, bf16[16,1920]{1,0:T(8,128)(2,1)S(1)}, u32[]{:S(2)}, u32[]{:S(2)}) collective-permute-start(bf16[16,1920]{1,0:T(8,128)(2,1)S(1)} %slice_bitcast_fusion.2), channel_id=1, source_target_pairs={{2,0},{3,1},{4,2},{5,3},{6,4},{7,5},{8,6},{9,7},{10,8},{11,9},{12,... | collective-permute-start | bytes 184328 | tf_op jit(solution)/shard_map/ppermute | solution.py:29
  89.0 20.7 %collective-permute-start.3 = (bf16[128,1920]{1,0:T(8,128)(2,1)S(1)}, bf16[128,1920]{1,0:T(8,128)(2,1)}, u32[]{:S(2)}, u32[]{:S(2)}) collective-permute-start(bf16[128,1920]{1,0:T(8,128)(2,1)S(1)} %fusion.6.own), channel_id=1, source_target_pairs={{0,1},{1,2},{2,3},{3,4},{4,5},{5,6},{6,7},{7,8},{8,9},{9,10},{10,1... | collective-permute-start | bytes 1474568 | tf_op jit(solution)/shard_map/ppermute | solution.py:29
  91.0 18.7 %collective-permute-start.4 = (bf16[128,1920]{1,0:T(8,128)(2,1)S(1)}, bf16[128,1920]{1,0:T(8,128)(2,1)}, u32[]{:S(2)}, u32[]{:S(2)}) collective-permute-start(bf16[128,1920]{1,0:T(8,128)(2,1)S(1)} %fusion.6.own), channel_id=1, source_target_pairs={{1,0},{2,1},{3,2},{4,3},{5,4},{6,5},{7,6},{8,7},{9,8},{10,9},{11,1... | collective-permute-start | bytes 1474568 | tf_op jit(solution)/shard_map/ppermute | solution.py:29
  93.0 8.2 %collective-permute-start.2 = (bf16[16,1920]{1,0:T(8,128)(2,1)}, bf16[16,1920]{1,0:T(8,128)(2,1)S(1)}, u32[]{:S(2)}, u32[]{:S(2)}) collective-permute-start(bf16[16,1920]{1,0:T(8,128)(2,1)} %get-tuple-element.76), channel_id=1, source_target_pairs={{0,2},{1,3},{2,4},{3,5},{4,6},{5,7},{6,8},{7,9},{8,10},{9,11},{10,... | collective-permute-start | bytes 184328 | tf_op jit(solution)/shard_map/ppermute | solution.py:29
  96.9 12.8 %collective-permute-start.5 = (bf16[16,1920]{1,0:T(8,128)(2,1)}, bf16[16,1920]{1,0:T(8,128)(2,1)S(1)}, u32[]{:S(2)}, u32[]{:S(2)}) collective-permute-start(bf16[16,1920]{1,0:T(8,128)(2,1)} %get-tuple-element.75), channel_id=1, source_target_pairs={{2,0},{3,1},{4,2},{5,3},{6,4},{7,5},{8,6},{9,7},{10,8},{11,9},{12,... | collective-permute-start | bytes 184328 | tf_op jit(solution)/shard_map/ppermute | solution.py:29
  100.0 43.4 %collective-permute-start.13 = (bf16[128,512]{0,1:T(8,128)(2,1)}, bf16[128,512]{0,1:T(8,128)(2,1)}, u32[]{:S(2)}, u32[]{:S(2)}) collective-permute-start(bf16[128,512]{0,1:T(8,128)(2,1)} %get-tuple-element.77), channel_id=1, source_target_pairs={{0,1},{1,0},{2,3},{3,2},{4,5},{5,4},{6,7},{7,6},{8,9},{9,8},{10,11... | collective-permute-start | bytes 393224 | tf_op jit(solution)/shard_map/ppermute | solution.py:33
  112.1 14.9 %copy-start.10 = (bf16[1024,1920]{1,0:T(8,128)(2,1)S(1)}, bf16[1024,1920]{1,0:T(8,128)(2,1)}, u32[]{:S(2)}) copy-start(bf16[1024,1920]{1,0:T(8,128)(2,1)} %param.14) | copy-start | bytes 11796484
  127.0 15.4 %collective-permute-start.12 = (bf16[128,1920]{1,0:T(8,128)(2,1)}, bf16[128,1920]{1,0:T(8,128)(2,1)}, u32[]{:S(2)}, u32[]{:S(2)}) collective-permute-start(bf16[128,1920]{1,0:T(8,128)(2,1)} %get-tuple-element.28), channel_id=1, source_target_pairs={{0,1},{1,0},{2,3},{3,2},{4,5},{5,4},{6,7},{7,6},{8,9},{9,8},{10,11... | collective-permute-start | bytes 1474568 | tf_op jit(solution)/shard_map/ppermute | solution.py:33
  130.3 27.1 %all-to-all-start.2 = ((bf16[8,176,128]{2,1,0:T(8,128)(2,1)}), bf16[8,176,128]{2,1,0:T(8,128)(2,1)S(1)}, u32[]{:S(2)}, u32[]{:S(2)}) async-start(bf16[8,176,128]{2,1,0:T(8,128)(2,1)} %pad_maximum_fusion.2), calls=%async_computation.2 | async-start | bytes 720896 | tf_op jit(solution)/shard_map/all_to_all | solution.py:37
  147.5 16.4 %copy-start.7 = (bf16[8,128,128]{2,1,0:T(8,128)(2,1)S(1)}, bf16[8,128,128]{2,1,0:T(8,128)(2,1)}, u32[]{:S(2)}) copy-start(bf16[8,128,128]{2,1,0:T(8,128)(2,1)} %copy-done.6) | copy-start | bytes 786436
  147.5 16.5 %copy-start.9 = (bf16[1024,128]{1,0:T(8,128)(2,1)S(1)}, bf16[1024,128]{1,0:T(8,128)(2,1)}, u32[]{:S(2)}) copy-start(bf16[1024,128]{1,0:T(8,128)(2,1)} %copy-done.8) | copy-start | bytes 786436
  151.6 21.2 %collective-permute-start.14 = (bf16[1920,128]{1,0:T(8,128)(2,1)}, bf16[1920,128]{1,0:T(8,128)(2,1)}, u32[]{:S(2)}, u32[]{:S(2)}) collective-permute-start(bf16[1920,128]{1,0:T(8,128)(2,1)} %convolution_convert_fusion.2), channel_id=1, source_target_pairs={{0,32},{32,64},{64,96},{96,0},{1,33},{33,65},{65,97},{97,1},{2,34}... | collective-permute-start | bytes 1474568 | tf_op jit(solution)/shard_map/ppermute | solution.py:502
  153.2 26.7 %collective-permute-start.15 = (bf16[1920,128]{1,0:T(8,128)(2,1)}, bf16[1920,128]{1,0:T(8,128)(2,1)}, u32[]{:S(2)}, u32[]{:S(2)}) collective-permute-start(bf16[1920,128]{1,0:T(8,128)(2,1)} %convolution_convert_fusion.1), channel_id=1, source_target_pairs={{0,64},{32,96},{64,0},{96,32},{1,65},{33,97},{65,1},{97,33},{2,66}... | collective-permute-start | bytes 1474568 | tf_op jit(solution)/shard_map/ppermute | solution.py:502
  156.1 23.8 %collective-permute-start.16 = (bf16[1920,128]{1,0:T(8,128)(2,1)}, bf16[1920,128]{1,0:T(8,128)(2,1)}, u32[]{:S(2)}, u32[]{:S(2)}) collective-permute-start(bf16[1920,128]{1,0:T(8,128)(2,1)} %convolution_convert_fusion), channel_id=1, source_target_pairs={{0,96},{32,0},{64,32},{96,64},{1,97},{33,1},{65,33},{97,65},{2,98}... | collective-permute-start | bytes 1474568 | tf_op jit(solution)/shard_map/ppermute | solution.py:502
  158.3 26.1 %all-to-all-start.3 = ((f32[8,48,128]{2,1,0:T(8,128)}), f32[8,48,128]{2,1,0:T(8,128)}, u32[]{:S(2)}, u32[]{:S(2)}) async-start(f32[8,48,128]{2,1,0:T(8,128)} %broadcast_in_dim.26), calls=%async_computation.3 | async-start | bytes 393216 | tf_op jit(solution)/shard_map/all_to_all | solution.py:37
  164.0 15.9 %copy-start.13 = (bf16[1920,128]{1,0:T(8,128)(2,1)S(1)}, bf16[1920,128]{1,0:T(8,128)(2,1)}, u32[]{:S(2)}) copy-start(bf16[1920,128]{1,0:T(8,128)(2,1)} %convolution_convert_fusion.3) | copy-start | bytes 1474564
  172.8 18.4 %collective-permute-start.8 = (bf16[2,2,512,256]{3,2,1,0:T(8,128)(2,1)}, bf16[2,2,512,256]{3,2,1,0:T(8,128)(2,1)}, u32[]{:S(2)}, u32[]{:S(2)}) collective-permute-start(bf16[2,2,512,256]{3,2,1,0:T(8,128)(2,1)} %get-tuple-element.33), channel_id=1, source_target_pairs={{0,1},{1,0},{2,3},{3,2},{4,5},{5,4},{6,7},{7,6},{8,9},{9,8},{10,11... | collective-permute-start | bytes 3145736 | tf_op jit(solution)/shard_map/ppermute | solution.py:33
  182.3 7.9 %collective-permute-start.17 = (bf16[16,60,128]{2,1,0:T(8,128)(2,1)}, bf16[16,60,128]{2,1,0:T(8,128)(2,1)S(1)}, u32[]{:S(2)}, u32[]{:S(2)}) collective-permute-start(bf16[16,60,128]{2,1,0:T(8,128)(2,1)} %fusion.9), channel_id=1, source_target_pairs={{0,0},{1,128},{128,1},{129,129},{2,2},{3,130},{130,3},{131,131},{4... | collective-permute-start | bytes 737288 | tf_op jit(solution)/shard_map/ppermute | solution.py:514
  184.3 6.9 %collective-permute-start.18 = (bf16[16,60,128]{2,1,0:T(8,128)(2,1)S(1)}, bf16[16,60,128]{2,1,0:T(8,128)(2,1)S(1)}, u32[]{:S(2)}, u32[]{:S(2)}) collective-permute-start(bf16[16,60,128]{2,1,0:T(8,128)(2,1)S(1)} %fusion.8), channel_id=1, source_target_pairs={{0,1},{1,129},{128,0},{129,128},{2,3},{3,131},{130,2},{131,130},{4... | collective-permute-start | bytes 737288 | tf_op jit(solution)/shard_map/ppermute | solution.py:514
  185.3 1.4 collective-permute-start.10
  186.8 8.2 %collective-permute-start.11 = (f32[48,128]{1,0:T(8,128)S(1)}, f32[48,128]{1,0:T(8,128)S(1)}, u32[]{:S(2)}, u32[]{:S(2)}) collective-permute-start(f32[48,128]{1,0:T(8,128)S(1)} %add.87), channel_id=1, source_target_pairs={{0,8},{8,0},{1,9},{9,1},{2,10},{10,2},{3,11},{11,3},{4,12},{12,4},... | collective-permute-start | bytes 73736 | tf_op jit(solution)/shard_map/ppermute | solution.py:33
  192.8 17.1 %collective-permute-start.9 = (bf16[2,512,256]{2,1,0:T(8,128)(2,1)S(1)}, bf16[2,512,256]{2,1,0:T(8,128)(2,1)S(1)}, u32[]{:S(2)}, u32[]{:S(2)}) collective-permute-start(bf16[2,512,256]{2,1,0:T(8,128)(2,1)S(1)} %fusion.7), channel_id=1, source_target_pairs={{0,8},{8,0},{1,9},{9,1},{2,10},{10,2},{3,11},{11,3},{4,12},{12,4},... | collective-permute-start | bytes 1572872 | tf_op jit(solution)/shard_map/ppermute | solution.py:33
  192.9 16.9 %collective-permute-start.19 = (bf16[2,4,60,128]{3,2,1,0:T(8,128)(2,1)S(1)}, bf16[2,4,60,128]{3,2,1,0:T(8,128)(2,1)S(1)}, u32[]{:S(2)}, u32[]{:S(2)}) collective-permute-start(bf16[2,4,60,128]{3,2,1,0:T(8,128)(2,1)S(1)} %fusion.11), channel_id=1, source_target_pairs={{0,8},{8,0},{1,9},{9,1},{2,10},{10,2},{3,11},{11,3},{4,12},{12,4},... | collective-permute-start | bytes 368648 | tf_op jit(solution)/shard_map/ppermute | solution.py:33
  (11 other events, 52.5 us)

commit v2 on v1

--- a/solution.py
+++ b/solution.py
@@ -65,11 +65,8 @@
 
 
 def hyena_kernel(
-    prev_far,
-    prev,
     own,
-    following,
-    following_far,
+    sides,
     x_all,
     cot_all,
     cot_next,
@@ -110,11 +107,9 @@
         reversed_sums[...] = jnp.zeros_like(reversed_sums)
         small[groups] = jnp.zeros((SMALL, FCH), f32)
 
-    ext[0:FAR, :] = prev_far[...].astype(f32)
-    ext[FAR:edge, :] = prev[...].astype(f32)
+    ext[0:edge, :] = sides[0:edge, :].astype(f32)
     ext[edge : edge + LONG, :] = own[...].astype(f32)
-    ext[edge + LONG : edge + 2 * LONG, :] = following[...].astype(f32)
-    ext[edge + 2 * LONG :, :] = following_far[...].astype(f32)
+    ext[edge + LONG :, :] = sides[edge:, :].astype(f32)
     cot_ext[0:LONG, :] = cot_all[:, columns].astype(f32)
     cot_ext[LONG : 2 * LONG, :] = cot_next[...].astype(f32)
     cot_ext[2 * LONG :, :] = cot_far[...].astype(f32)
@@ -233,11 +228,8 @@
         hyena_kernel,
         grid=(FILTERS,),
         in_specs=[
-            part(FAR),
             part(rows),
-            part(rows),
-            part(rows),
-            part(FAR),
+            part(2 * edge),
             whole((rows, D)),
             whole((rows, D)),
             part(rows),
@@ -279,11 +271,8 @@
             flops=2 * 4 * 1024 * 1024 * 60, bytes_accessed=12 * 1024 * 1024, transcendentals=0
         ),
     )(
-        sides[0],
-        sides[1],
         normed,
-        sides[2],
-        sides[3],
+        sides,
         x_first,
         cotangent,
         cot_sides[0],
@@ -320,22 +309,33 @@
     return logits
 
 
-def attend_kernel(place, query, kv, out, log_total, top, total, wide):
+def key_rows(parts, span):
+    ref = parts[span // 2 % 2][span % 2]
+    first = span // 4 * 4
+    keys = ref[first : first + 4, 0:LONG, :].reshape(SPAN, HDIM)
+    values = ref[first : first + 4, LONG:, :].reshape(SPAN, HDIM)
+    return keys, values
+
+
+def attend_kernel(
+    place, query, own, far, own_c, far_c, out, log_total, top, total, wide
+):
+    parts = ((own, far), (own_c, far_c))
     f32 = jnp.float32
     for half in range(2):
         q_rows = query[half * SPAN : (half + 1) * SPAN, :]
         for span, kind in spans_of(half):
 
             def visit(span=span, kind=kind):
-                rows = slice(span * SPAN, (span + 1) * SPAN)
-                logits = logits_of(kv[rows, 0:HDIM], q_rows, kind, place[1])
+                k_rows, v_rows = key_rows(parts, span)
+                logits = logits_of(k_rows, q_rows, kind, place[1])
                 high = jnp.max(logits, axis=0, keepdims=True)
                 if kind > 0:
                     high = jnp.maximum(high, top[...])
                 probs = jnp.exp(logits - high)
                 part = jnp.sum(probs, axis=0, keepdims=True)
                 values = lax.dot_general(
-                    kv[rows, HDIM:],
+                    v_rows,
                     probs.astype(jnp.bfloat16),
                     (((0,), (0,)), ((), ())),
                     preferred_element_type=f32,
@@ -361,11 +361,8 @@
     count = query.shape[0]
     return pl.pallas_call(
         attend_kernel,
-        in_specs=[
-            pl.BlockSpec(memory_space=pltpu.SMEM),
-            pl.BlockSpec(memory_space=pltpu.VMEM),
-            pl.BlockSpec(memory_space=pltpu.VMEM),
-        ],
+        in_specs=[pl.BlockSpec(memory_space=pltpu.SMEM)]
+        + [pl.BlockSpec(memory_space=pltpu.VMEM)] * 5,
         out_shape=[
             jax.ShapeDtypeStruct((count, HDIM), jnp.bfloat16),
             jax.ShapeDtypeStruct((1, count), jnp.float32),
@@ -379,12 +376,26 @@
         cost_estimate=pl.CostEstimate(
             flops=1600000000, bytes_accessed=3000000, transcendentals=3000000
         ),
-    )(place, query, kv)
+    )(place, query, *kv)
 
 
 def attend_back_kernel(
-    place, query, kv, out, log_total, grad_out, grad_query, same_core, other_core, sums, wide
+    place,
+    query,
+    own,
+    far,
+    own_c,
+    far_c,
+    out,
+    log_total,
+    grad_out,
+    grad_query,
+    same_core,
+    other_core,
+    sums,
+    wide,
 ):
+    parts = ((own, far), (own_c, far_c))
     f32 = jnp.float32
     low = jnp.bfloat16
     scale = HDIM**-0.5
@@ -399,12 +410,12 @@
             rows = slice(span * SPAN, (span + 1) * SPAN)
             fresh = half == 1 and span >= 4 or half == 0
 
-            def visit(rows=rows, kind=kind, fresh=fresh):
-                k_rows = kv[rows, 0:HDIM]
+            def visit(rows=rows, span=span, kind=kind, fresh=fresh):
+                k_rows, v_rows = key_rows(parts, span)
                 logits = logits_of(k_rows, q_rows, kind, place[1])
                 probs = jnp.exp(logits - log_row)
                 grad_probs = lax.dot_general(
-                    kv[rows, HDIM:],
+                    v_rows,
                     g_rows,
                     (((1,), (1,)), ((), ())),
                     preferred_element_type=f32,
@@ -446,17 +457,37 @@
     part = jax.ShapeDtypeStruct((2, 2, SPAN, 2 * HDIM), jnp.bfloat16)
     return pl.pallas_call(
         attend_back_kernel,
-        in_specs=[pl.BlockSpec(memory_space=pltpu.SMEM)] + [vmem] * 5,
+        in_specs=[pl.BlockSpec(memory_space=pltpu.SMEM)] + [vmem] * 8,
         out_shape=[jax.ShapeDtypeStruct(query.shape, jnp.bfloat16), part, part],
         scratch_shapes=[
-            pltpu.VMEM(kv.shape, jnp.float32),
+            pltpu.VMEM((8 * SPAN, 2 * HDIM), jnp.float32),
             pltpu.VMEM((HDIM, SPAN), jnp.float32),
         ],
         compiler_params=pltpu.CompilerParams(vmem_limit_bytes=40 * 1024 * 1024),
         cost_estimate=pl.CostEstimate(
             flops=4000000000, bytes_accessed=6000000, transcendentals=3000000
         ),
-    )(place, query, kv, out, log_total, grad_out)
+    )(place, query, *kv, out, log_total, grad_out)
+
+
+def both_sides(rows):
+    return (
+        from_behind(rows[-FAR:], 2),
+        from_behind(rows, 1),
+        from_behind(rows, -1),
+        from_behind(rows[:FAR], -2),
+    )
+
+
+def first_norm(residual, attention, w_out, norm_gain):
+    x_float = residual.astype(jnp.float32) + jnp.dot(
+        attention, w_out, preferred_element_type=jnp.float32
+    )
+    x_first = lax.optimization_barrier(x_float.astype(jnp.bfloat16))
+    x_float = x_first.astype(jnp.float32)
+    inv_rms = lax.rsqrt(jnp.mean(x_float * x_float, axis=-1, keepdims=True) + 1e-05)
+    normed = lax.optimization_barrier((x_float * inv_rms * norm_gain).astype(jnp.bfloat16))
+    return x_first, inv_rms, normed
 
 
 def to_heads(rows_in):
@@ -467,11 +498,9 @@
     return pieces.transpose(1, 0, 2).reshape(pieces.shape[1], HEADS * HDIM)
 
 
-def gather_keys(kv_own):
-    wide = jnp.stack([kv_own, swap(kv_own, "xb")])
-    both = jnp.stack([wide, swap(wide, "c")])
-    both = both.reshape(2, 2, 2, 4, 2, -1, HDIM).transpose(2, 0, 1, 3, 5, 4, 6)
-    return both.reshape(-1, 2 * HDIM)
+def gather_keys(own):
+    far = swap(own, "xb")
+    return own, far, swap(own, "c"), swap(far, "c")
 
 
 def weight_pieces(attention, grad_residual):
@@ -538,29 +567,24 @@
 ):
     tok_rows = query_in.shape[1]
     matrices = toeplitz(filters)
-    cot_sides = (from_behind(cotangent[0], -1), from_behind(cotangent[0, :FAR], -2))
     qkv_send = jnp.concatenate(
         [to_heads(query_in[0]), to_heads(key_in[0]), to_heads(value_in[0])], axis=1
     )
     qkv_own = exchange(qkv_send, HEAD_AXES)
     query_rows = qkv_own[:, :tok_rows].reshape(8 * tok_rows, HDIM)
     kv_all = gather_keys(qkv_own[:, tok_rows:])
+    apart = lax.optimization_barrier((residual[0], cotangent[0], qkv_own))
+    res_sides = both_sides(apart[0])
+    cot_sides = (from_behind(apart[1], -1), from_behind(apart[1][:FAR], -2))
     query_total = 8 * tok_rows
     place = jnp.stack([lax.axis_index("xb"), lax.axis_index("c")]).astype(jnp.int32)
     head_out, log_total = attend(place, query_rows, kv_all)
+    head_out, res_sides, cot_sides = lax.optimization_barrier((head_out, res_sides, cot_sides))
     attention = from_heads(exchange(head_out.reshape(8, tok_rows, HDIM), HEAD_AXES))
-    x_float = residual[0].astype(jnp.float32) + jnp.dot(
-        attention, w_out, preferred_element_type=jnp.float32
-    )
-    x_first = lax.optimization_barrier(x_float.astype(jnp.bfloat16))
-    x_float = x_first.astype(jnp.float32)
-    inv_rms = lax.rsqrt(jnp.mean(x_float * x_float, axis=-1, keepdims=True) + 1e-05)
-    normed = lax.optimization_barrier((x_float * inv_rms * norm_gain).astype(jnp.bfloat16))
-    sides = (
-        from_behind(normed[tok_rows - FAR :], 2),
-        from_behind(normed, 1),
-        from_behind(normed, -1),
-        from_behind(normed[:FAR], -2),
+    att_sides = both_sides(attention)
+    x_first, inv_rms, normed = first_norm(residual[0], attention, w_out, norm_gain)
+    _, _, sides = first_norm(
+        jnp.concatenate(res_sides), jnp.concatenate(att_sides), w_out, norm_gain
     )
     layer_out, grad_residual, small = hyena(
         normed,
@@ -586,6 +610,13 @@
     weight_part = weight_over_y(weight_pieces(attention, grad_residual))
     grad_rows_all = grad_recv[:, :tok_rows].reshape(query_total, HDIM)
     small_part = jnp.sum(grad_recv[:, tok_rows:].astype(jnp.float32), axis=0)
+    grad_query, same_core, other_core = attend_back(
+        place, query_rows, kv_all, head_out, log_total, grad_rows_all
+    )
+    dq_send = grad_query.reshape(8, tok_rows, HDIM)
+    dkv = same_core.astype(jnp.float32) + swap(other_core, "c").astype(jnp.float32)
+    dkv_far = swap(dkv[:, 1].astype(jnp.bfloat16), "xb")
+    small_part, _ = lax.optimization_barrier((small_part, grad_query))
     sequences = lax.axis_size(DP_AXES)
     small_part = exchange(
         jnp.broadcast_to(small_part[None], (sequences,) + small_part.shape), DP_AXES
@@ -594,14 +625,9 @@
     small_part = small_part + swap(small_part, "c")
     small_part = small_part + swap(small_part, "xb")
     small_part = small_part.astype(jnp.bfloat16)
-
-    grad_query, same_core, other_core = attend_back(
-        place, query_rows, kv_all, head_out, log_total, grad_rows_all
-    )
-    dq_send = grad_query.reshape(8, tok_rows, HDIM)
-    dkv = same_core.astype(jnp.float32) + swap(other_core, "c").astype(jnp.float32)
     weight_part = weight_over_zl(weight_part)
-    dkv = dkv[:, 0] + swap(dkv[:, 1].astype(jnp.bfloat16), "xb").astype(jnp.float32)
+    weight_part, _ = lax.optimization_barrier((weight_part, dkv_far))
+    dkv = dkv[:, 0] + dkv_far.astype(jnp.float32)
     dkv = dkv.reshape(8, tok_rows, 2 * HDIM).astype(jnp.bfloat16)
     weight_part = weight_over_xb(weight_part)
     weight_rows = weight_part.size // (8 * HDIM)

time: 256 us -> 278 us (1.086)
  starting transfers between devices: 45.3 us -> 69.1 us
  local copies, waits for them, and re-layouts: 26.3 us -> 20.4 us
  matrix products: 13.7 us -> 17.9 us
  waiting for transfers between devices: 55.9 us -> 59.8 us
  blocking collectives: 72.6 us -> 69.8 us
    ppermute x6 -> x10, starting transfers between devices: 11.3 us -> 22.8 us  [from_behind(): return lax.ppermute(x, CTX_AXES, pairs)]
    all_to_all x3, starting transfers between devices: 22.5 us -> 33.1 us  [exchange(): return lax.all_to_all(x, axes, split_axis=0, concat_axis=0, tiled=True)]
    all_to_all x3, waiting for transfers between devices: 8.39 us -> 17.8 us  [exchange(): return lax.all_to_all(x, axes, split_axis=0, concat_axis=0, tiled=True)]
    ppermute x3, waiting for transfers between devices: 7.06 us -> 0.01 us  [weight_over_y(): total = total + lax.ppermute(pieces[step], 'y', pairs).astype(jnp.float32)]
    dot_general x1 -> x2, matrix products: 3.05 us -> 7.27 us  [first_norm(): jnp.dot(attention, w_out, preferred_element_type=jnp.float32)]
    ppermute x6 -> x10, waiting for transfers between devices: 9.6 us -> 12.9 us  [from_behind(): return lax.ppermute(x, CTX_AXES, pairs)]
    unnamed x56 -> x59, local copies, waits for them, and re-layouts: 13 us -> 9.77 us
    all_to_all x2, blocking collectives: 72.6 us -> 69.8 us  [exchange(): return lax.all_to_all(x, axes, split_axis=0, concat_axis=0, tiled=True)]
  transfers between devices with their start and end apart: 23 -> 28, of which waited for: 9 -> 11; matrix products, arithmetic and copies ran while one was open for 14% -> 13% of each run, Pallas kernels for 11% -> 10%
where the time goes in v2:
time: 278 us; the launch traced here: 276 us
  blocking collectives  69.8 us (25%)
  starting transfers between devices  69.1 us (25%)
  waiting for transfers between devices  59.8 us (22%)
  Pallas kernels  27.4 us (10%)
  local copies, waits for them, and re-layouts  20.4 us (7%)
  matrix products  17.9 us (6%)
  other arithmetic  10.2 us (4%)
    all_to_all x2, blocking collectives, exchange(): return lax.all_to_all(x, axes, split_axis=0, concat_axis=0, tiled=True)  69.8 us
    all_to_all x3, starting transfers between devices, exchange(): return lax.all_to_all(x, axes, split_axis=0, concat_axis=0, tiled=True)  33.1 us
    ppermute x10, waiting for transfers between devices, swap(): return lax.ppermute(x, axis, [(0, 1), (1, 0)])  26.8 us
    ppermute x10, starting transfers between devices, from_behind(): return lax.ppermute(x, CTX_AXES, pairs)  22.8 us
    all_to_all x3, waiting for transfers between devices, exchange(): return lax.all_to_all(x, axes, split_axis=0, concat_axis=0, tiled=True)  17.8 us
    pallas_call x1, Pallas kernels, hyena(): pl.pallas_call(hyena_kernel, grid=(FILTERS,), in_specs=[part(rows), part(...  13.9 us
    ppermute x10, waiting for transfers between devices, from_behind(): return lax.ppermute(x, CTX_AXES, pairs)  12.9 us
    unnamed x59, local copies, waits for them, and re-layouts  9.77 us
  transfers between devices with their start and end apart: 28, of which 11 were waited for; matrix products, arithmetic and copies ran while one was open for 13% of the time, Pallas kernels for 10%

profile of v2, /device:TPU:32, one launch (start us, length us, event | category | flops | bytes accessed | tf_op | source)
XLA Modules:
  0.0 275.9 jit_solution(16824035332638293820)
XLA Ops:
  3.8 35.0 %all_to_all.25 = bf16[8,384,128]{2,1,0:T(8,128)(2,1)S(1)} all-to-all(bf16[8,384,128]{2,1,0:T(8,128)(2,1)S(1)} %pad_maximum_fusion), channel_id=1, replica_groups=mesh['zl'=2,'y'=4,'xa'=2,'xb'=2,'zh'=4,'c'=2] {'xa','zh'}, dimensions={0} | all-to-all | bytes 1572864 | tf_op jit(solution)/shard_map/all_to_all | solution.py:37
  39.5 10.9 %collective-permute-done.far = bf16[8,256,128]{2,1,0:T(8,128)(2,1)S(1)} collective-permute-done((bf16[8,256,128]{2,1,0:T(8,128)(2,1)S(1)}, bf16[8,256,128]{2,1,0:T(8,128)(2,1)S(1)}, u32[]{:S(2)}, u32[]{:S(2)}) %collective-permute-start) | collective-permute-done | bytes 524320 | tf_op jit(solution)/shard_map/ppermute | solution.py:33
  51.4 2.8 %collective-permute-start.3 = (bf16[16,1920]{1,0:T(8,128)(2,1)S(1)}, bf16[16,1920]{1,0:T(8,128)(2,1)}, u32[]{:S(2)}, u32[]{:S(2)}) collective-permute-start(bf16[16,1920]{1,0:T(8,128)(2,1)S(1)} %get-tuple-element.96), channel_id=1, source_target_pairs={{0,2},{1,3},{2,4},{3,5},{4,6},{5,7},{6,8},{7,9},{8,10},{9,11},{10,... | collective-permute-start | bytes 184328 | tf_op jit(solution)/shard_map/ppermute | solution.py:29
  54.2 2.8 %collective-permute-start.4 = (bf16[128,1920]{1,0:T(8,128)(2,1)}, bf16[128,1920]{1,0:T(8,128)(2,1)}, u32[]{:S(2)}, u32[]{:S(2)}) collective-permute-start(bf16[128,1920]{1,0:T(8,128)(2,1)} %bitcast), channel_id=1, source_target_pairs={{0,1},{1,2},{2,3},{3,4},{4,5},{5,6},{6,7},{7,8},{8,9},{9,10},{10,1... | collective-permute-start | bytes 1474568 | tf_op jit(solution)/shard_map/ppermute | solution.py:29
  63.4 5.5 %shard_map.177 = (bf16[1024,128]{1,0:T(8,128)(2,1)S(1)}, f32[1,1024]{1,0:T(1,128)S(1)}) custom-call(s32[2]{0:T(128)S(1)} %pad_add_fusion.place, bf16[1024,128]{1,0:T(8,128)(2,1)S(1)} %bitcast.116, bf16[8,256,128]{2,1,0:T(8,128)(2,1)S(1)} %slice.141.own, bf16[8,256,128]{2,1,0:T(8,128)(2,1)S(1)} %collective-permute-done.far, ...), custom_call_target="tpu_custom_call" | custom-call | flops 1600000000 | bytes 3000000 | tf_op jit(solution)/shard_map/pallas_call | solution.py:362
  68.9 8.8 %collective-permute-done.6 = bf16[16,1920]{1,0:T(8,128)(2,1)S(1)} collective-permute-done((bf16[16,1920]{1,0:T(8,128)(2,1)S(1)}, bf16[16,1920]{1,0:T(8,128)(2,1)S(1)}, u32[]{:S(2)}, u32[]{:S(2)}) %collective-permute-start.6) | collective-permute-done | bytes 61472 | tf_op jit(solution)/shard_map/ppermute | solution.py:29
  79.3 17.7 %all-to-all-start.1 = ((bf16[8,128,128]{1,2,0:T(8,128)(2,1)}), bf16[8,128,128]{1,2,0:T(8,128)(2,1)}, u32[]{:S(2)}, u32[]{:S(2)}) async-start(bf16[8,128,128]{1,2,0:T(8,128)(2,1)} %copy.122), calls=%async_computation.1 | async-start | bytes 524288 | tf_op jit(solution)/shard_map/all_to_all | solution.py:37
  98.9 10.7 %all-to-all-done.1 = bf16[8,128,128]{1,2,0:T(8,128)(2,1)} async-done(((bf16[8,128,128]{1,2,0:T(8,128)(2,1)}), bf16[8,128,128]{1,2,0:T(8,128)(2,1)}, u32[]{:S(2)}, u32[]{:S(2)}) %all-to-all-start.1) | async-done | bytes 262176 | tf_op jit(solution)/shard_map/all_to_all | solution.py:37
  109.6 2.0 collective-permute-start.10
  112.9 1.9 fusion.44
  116.0 7.4 %collective-permute-start.9 = (bf16[16,1024]{0,1:T(8,128)(2,1)}, bf16[16,1024]{0,1:T(8,128)(2,1)}, u32[]{:S(2)}, u32[]{:S(2)}) collective-permute-start(bf16[16,1024]{0,1:T(8,128)(2,1)} %bitcast.14), channel_id=1, source_target_pairs={{0,2},{1,3},{2,4},{3,5},{4,6},{5,7},{6,8},{7,9},{8,10},{9,11},{10,... | collective-permute-start | bytes 98312 | tf_op jit(solution)/shard_map/ppermute | solution.py:29
  123.5 3.0 %fusion.1.x_all = bf16[128,1920]{1,0:T(8,128)(2,1)S(1)} fusion(bf16[128,1024]{0,1:T(8,128)(2,1)} %bitcast.13, bf16[1024,1920]{1,0:T(8,128)(2,1)} %param.14, bf16[1,128,1920]{2,1,0:T(8,128)(2,1)} %param.13), kind=kOutput, calls=%fused_computation.5 | convolution fusion | flops 504053760 | bytes 5177344 | tf_op jit(solution)/shard_map/dot_general | solution.py:483
  130.2 3.4 %collective-permute-done.9 = bf16[16,1024]{0,1:T(8,128)(2,1)} collective-permute-done((bf16[16,1024]{0,1:T(8,128)(2,1)}, bf16[16,1024]{0,1:T(8,128)(2,1)}, u32[]{:S(2)}, u32[]{:S(2)}) %collective-permute-start.9) | collective-permute-done | bytes 32800 | tf_op jit(solution)/shard_map/ppermute | solution.py:29
  133.6 4.2 %fusion = bf16[288,1920]{1,0:T(8,128)(2,1)S(1)} fusion(bf16[1024,1920]{1,0:T(8,128)(2,1)} %param.14, bf16[16,1920]{1,0:T(8,128)(2,1)} %copy-done.21, bf16[128,1920]{1,0:T(8,128)(2,1)} %collective-permute-done.5, bf16[128,1920]{1,0:T(8,128)(2,1)} %collective-permute-done.4, bf16[16,1920]{1,0:T(8,128)(2,1)} %collective-permute-done.3, ...), kind=kOutput, calls=%fused_computation.3 | convolution fusion | flops 1140350976 | bytes 6733824 | tf_op jit(solution)/shard_map/dot_general | solution.py:483
  139.0 13.9 %shard_map.179 = (bf16[128,1920]{1,0:T(8,128)(2,1)}, bf16[128,1920]{1,0:T(8,128)(2,1)}, f32[16,24,128]{2,1,0:T(8,128)S(1)}) custom-call(bf16[128,1920]{1,0:T(8,128)(2,1)S(1)} %fusion.10.own, bf16[288,1920]{1,0:T(8,128)(2,1)S(1)} %fusion.4.sides, bf16[128,1920]{1,0:T(8,128)(2,1)S(1)} %fusion.1.x_all, bf16[128,1920]{1,0:T(8,128)(2,1)S(1)} %bitcast.115, ...), custom_call_target="tpu_custom_call" | custom-call | flops 503316480 | bytes 12582912 | tf_op jit(solution)/shard_map/pallas_call | solution.py:227
  152.9 2.4 fusion.5
  156.2 9.4 %all-to-all-start.2 = ((bf16[8,176,128]{2,1,0:T(8,128)(2,1)}), bf16[8,176,128]{2,1,0:T(8,128)(2,1)S(1)}, u32[]{:S(2)}, u32[]{:S(2)}) async-start(bf16[8,176,128]{2,1,0:T(8,128)(2,1)} %pad_maximum_fusion.1), calls=%async_computation.2 | async-start | bytes 720896 | tf_op jit(solution)/shard_map/all_to_all | solution.py:37
  165.8 2.0 convolution_convert_fusion
  167.8 2.0 convolution_convert_fusion.1
  169.8 2.1 convolution_convert_fusion.2
  171.9 2.0 convolution_convert_fusion.3
  175.5 2.9 %collective-permute-start.20 = (bf16[1920,128]{1,0:T(8,128)(2,1)}, bf16[1920,128]{1,0:T(8,128)(2,1)}, u32[]{:S(2)}, u32[]{:S(2)}) collective-permute-start(bf16[1920,128]{1,0:T(8,128)(2,1)} %convolution_convert_fusion.1), channel_id=1, source_target_pairs={{0,64},{32,96},{64,0},{96,32},{1,65},{33,97},{65,1},{97,33},{2,66}... | collective-permute-start | bytes 1474568 | tf_op jit(solution)/shard_map/ppermute | solution.py:531
  184.3 7.4 %shard_map.180 = (bf16[1024,128]{1,0:T(8,128)(2,1)S(1)}, bf16[2,2,512,256]{3,2,1,0:T(8,128)(2,1)S(1)}, bf16[2,2,512,256]{3,2,1,0:T(8,128)(2,1)S(1)}) custom-call(s32[2]{0:T(128)S(1)} %pad_add_fusion.place, bf16[1024,128]{1,0:T(8,128)(2,1)S(1)} %bitcast.117, bf16[8,256,128]{2,1,0:T(8,128)(2,1)S(1)} %copy-done.3, bf16[8,256,128]{2,1,0:T(8,128)(2,1)S(1)} %copy-done.9, ...), custom_call_target="tpu_custom_call" | custom-call | flops 4000000000 | bytes 6000000 | tf_op jit(solution)/shard_map/pallas_call | solution.py:458
  193.3 5.9 %all-to-all-start.3 = ((f32[8,48,128]{2,1,0:T(8,128)}), f32[8,48,128]{2,1,0:T(8,128)S(1)}, u32[]{:S(2)}, u32[]{:S(2)}) async-start(f32[8,48,128]{2,1,0:T(8,128)} %broadcast_in_dim.13), calls=%async_computation.3 | async-start | bytes 393216 | tf_op jit(solution)/shard_map/all_to_all | solution.py:37
  199.2 5.5 %all-to-all-done.3 = f32[8,48,128]{2,1,0:T(8,128)S(1)} async-done(((f32[8,48,128]{2,1,0:T(8,128)}), f32[8,48,128]{2,1,0:T(8,128)S(1)}, u32[]{:S(2)}, u32[]{:S(2)}) %all-to-all-start.3) | async-done | bytes 196640 | tf_op jit(solution)/shard_map/all_to_all | solution.py:37
  204.9 2.5 add_convert_fusion
  208.6 3.4 %collective-permute-start.22 = (bf16[16,60,128]{2,1,0:T(8,128)(2,1)S(1)}, bf16[16,60,128]{2,1,0:T(8,128)(2,1)S(1)}, u32[]{:S(2)}, u32[]{:S(2)}) collective-permute-start(bf16[16,60,128]{2,1,0:T(8,128)(2,1)S(1)} %fusion.20), channel_id=1, source_target_pairs={{0,0},{1,128},{128,1},{129,129},{2,2},{3,130},{130,3},{131,131},{4... | collective-permute-start | bytes 737288 | tf_op jit(solution)/shard_map/ppermute | solution.py:543
  212.2 2.3 collective-permute-start.16
  216.4 2.3 collective-permute-done.23
  218.8 11.3 %collective-permute-done.14 = bf16[2,512,256]{2,1,0:T(8,128)(2,1)S(1)} collective-permute-done((bf16[2,512,256]{2,1,0:T(8,128)(2,1)S(1)}, bf16[2,512,256]{2,1,0:T(8,128)(2,1)S(1)}, u32[]{:S(2)}, u32[]{:S(2)}) %collective-permute-start.14) | collective-permute-done | bytes 524320 | tf_op jit(solution)/shard_map/ppermute | solution.py:33
  230.8 4.3 %collective-permute-done.24 = bf16[2,4,60,128]{3,2,1,0:T(8,128)(2,1)S(1)} collective-permute-done((bf16[2,4,60,128]{3,2,1,0:T(8,128)(2,1)S(1)}, bf16[2,4,60,128]{3,2,1,0:T(8,128)(2,1)S(1)}, u32[]{:S(2)}, u32[]{:S(2)}) %collective-permute-start.24) | collective-permute-done | bytes 122912 | tf_op jit(solution)/shard_map/ppermute | solution.py:33
  235.3 34.8 %all_to_all.26 = bf16[8,492,128]{2,1,0:T(8,128)(2,1)S(1)} all-to-all(bf16[8,492,128]{2,1,0:T(8,128)(2,1)S(1)} %constant_dynamic-update-slice_fusion.2), channel_id=1, replica_groups=mesh['zl'=2,'y'=4,'xa'=2,'xb'=2,'zh'=4,'c'=2] {'xa','zh'}, dimensions={0} | all-to-all | bytes 2015232 | tf_op jit(solution)/shard_map/all_to_all | solution.py:37
  (153 shorter events, 41.6 us)
Async XLA Ops:
  3.7 54.6 %copy-start = (bf16[1,128,1920]{2,1,0:T(8,128)(2,1)S(1)}, bf16[1,128,1920]{2,1,0:T(8,128)(2,1)}, u32[]{:S(2)}) copy-start(bf16[1,128,1920]{2,1,0:T(8,128)(2,1)} %param.19) | copy-start | bytes 1474564
  38.8 11.6 %collective-permute-start = (bf16[8,256,128]{2,1,0:T(8,128)(2,1)S(1)}, bf16[8,256,128]{2,1,0:T(8,128)(2,1)S(1)}, u32[]{:S(2)}, u32[]{:S(2)}) collective-permute-start(bf16[8,256,128]{2,1,0:T(8,128)(2,1)S(1)} %slice.141.own), channel_id=1, source_target_pairs={{0,8},{8,0},{1,9},{9,1},{2,10},{10,2},{3,11},{11,3},{4,12},{12,4},... | collective-permute-start | bytes 1572872 | tf_op jit(solution)/shard_map/ppermute | solution.py:33
  39.5 21.2 %collective-permute-start.1 = (bf16[8,256,128]{2,1,0:T(8,128)(2,1)S(1)}, bf16[8,256,128]{2,1,0:T(8,128)(2,1)S(1)}, u32[]{:S(2)}, u32[]{:S(2)}) collective-permute-start(bf16[8,256,128]{2,1,0:T(8,128)(2,1)S(1)} %slice.141.own), channel_id=1, source_target_pairs={{0,1},{1,0},{2,3},{3,2},{4,5},{5,4},{6,7},{7,6},{8,9},{9,8},{10,11... | collective-permute-start | bytes 1572872 | tf_op jit(solution)/shard_map/ppermute | solution.py:33
  50.4 11.6 %collective-permute-start.2 = (bf16[8,256,128]{2,1,0:T(8,128)(2,1)S(1)}, bf16[8,256,128]{2,1,0:T(8,128)(2,1)}, u32[]{:S(2)}, u32[]{:S(2)}) collective-permute-start(bf16[8,256,128]{2,1,0:T(8,128)(2,1)S(1)} %collective-permute-done.far), channel_id=1, source_target_pairs={{0,1},{1,0},{2,3},{3,2},{4,5},{5,4},{6,7},{7,6},{8,9},{9,8},{10,11... | collective-permute-start | bytes 1572872 | tf_op jit(solution)/shard_map/ppermute | solution.py:33
  51.4 6.9 %collective-permute-start.3 = (bf16[16,1920]{1,0:T(8,128)(2,1)S(1)}, bf16[16,1920]{1,0:T(8,128)(2,1)}, u32[]{:S(2)}, u32[]{:S(2)}) collective-permute-start(bf16[16,1920]{1,0:T(8,128)(2,1)S(1)} %get-tuple-element.96), channel_id=1, source_target_pairs={{0,2},{1,3},{2,4},{3,5},{4,6},{5,7},{6,8},{7,9},{8,10},{9,11},{10,... | collective-permute-start | bytes 184328 | tf_op jit(solution)/shard_map/ppermute | solution.py:29
  54.2 24.2 %collective-permute-start.4 = (bf16[128,1920]{1,0:T(8,128)(2,1)}, bf16[128,1920]{1,0:T(8,128)(2,1)}, u32[]{:S(2)}, u32[]{:S(2)}) collective-permute-start(bf16[128,1920]{1,0:T(8,128)(2,1)} %bitcast), channel_id=1, source_target_pairs={{0,1},{1,2},{2,3},{3,4},{4,5},{5,6},{6,7},{7,8},{8,9},{9,10},{10,1... | collective-permute-start | bytes 1474568 | tf_op jit(solution)/shard_map/ppermute | solution.py:29
  57.0 21.4 %collective-permute-start.5 = (bf16[128,1920]{1,0:T(8,128)(2,1)}, bf16[128,1920]{1,0:T(8,128)(2,1)}, u32[]{:S(2)}, u32[]{:S(2)}) collective-permute-start(bf16[128,1920]{1,0:T(8,128)(2,1)} %bitcast), channel_id=1, source_target_pairs={{1,0},{2,1},{3,2},{4,3},{5,4},{6,5},{7,6},{8,7},{9,8},{10,9},{11,1... | collective-permute-start | bytes 1474568 | tf_op jit(solution)/shard_map/ppermute | solution.py:29
  58.3 20.1 %collective-permute-start.7 = (bf16[128,1920]{1,0:T(8,128)(2,1)S(1)}, bf16[128,1920]{1,0:T(8,128)(2,1)S(1)}, u32[]{:S(2)}, u32[]{:S(2)}) collective-permute-start(bf16[128,1920]{1,0:T(8,128)(2,1)S(1)} %bitcast.113), channel_id=1, source_target_pairs={{1,0},{2,1},{3,2},{4,3},{5,4},{6,5},{7,6},{8,7},{9,8},{10,9},{11,1... | collective-permute-start | bytes 1474568 | tf_op jit(solution)/shard_map/ppermute | solution.py:29
  60.7 17.0 %collective-permute-start.6 = (bf16[16,1920]{1,0:T(8,128)(2,1)S(1)}, bf16[16,1920]{1,0:T(8,128)(2,1)S(1)}, u32[]{:S(2)}, u32[]{:S(2)}) collective-permute-start(bf16[16,1920]{1,0:T(8,128)(2,1)S(1)} %get-tuple-element.95), channel_id=1, source_target_pairs={{2,0},{3,1},{4,2},{5,3},{6,4},{7,5},{8,6},{9,7},{10,8},{11,9},{12,... | collective-permute-start | bytes 184328 | tf_op jit(solution)/shard_map/ppermute | solution.py:29
  62.0 16.4 %collective-permute-start.8 = (bf16[16,1920]{1,0:T(8,128)(2,1)S(1)}, bf16[16,1920]{1,0:T(8,128)(2,1)S(1)}, u32[]{:S(2)}, u32[]{:S(2)}) collective-permute-start(bf16[16,1920]{1,0:T(8,128)(2,1)S(1)} %slice.111), channel_id=1, source_target_pairs={{2,0},{3,1},{4,2},{5,3},{6,4},{7,5},{8,6},{9,7},{10,8},{11,9},{12,... | collective-permute-start | bytes 184328 | tf_op jit(solution)/shard_map/ppermute | solution.py:29
  63.3 33.7 %copy-start.19 = (bf16[15,128]{1,0:T(8,128)(2,1)S(1)}, bf16[15,128]{1,0:T(8,128)(2,1)}, u32[]{:S(2)}) copy-start(bf16[15,128]{1,0:T(8,128)(2,1)} %param.17) | copy-start | bytes 11524
  63.3 34.8 %copy-start.18 = (f32[1920]{0:T(1024)S(1)}, f32[1920]{0:T(1024)}, u32[]{:S(2)}) copy-start(f32[1920]{0:T(1024)} %param.15) | copy-start | bytes 23044
  63.3 34.8 %copy-start.20 = (f32[1920]{0:T(1024)S(1)}, f32[1920]{0:T(1024)}, u32[]{:S(2)}) copy-start(f32[1920]{0:T(1024)} %param.18) | copy-start | bytes 23044
  79.3 30.3 %all-to-all-start.1 = ((bf16[8,128,128]{1,2,0:T(8,128)(2,1)}), bf16[8,128,128]{1,2,0:T(8,128)(2,1)}, u32[]{:S(2)}, u32[]{:S(2)}) async-start(bf16[8,128,128]{1,2,0:T(8,128)(2,1)} %copy.122), calls=%async_computation.1 | async-start | bytes 524288 | tf_op jit(solution)/shard_map/all_to_all | solution.py:37
  109.6 24.0 %collective-permute-start.10 = (bf16[128,1024]{0,1:T(8,128)(2,1)}, bf16[128,1024]{0,1:T(8,128)(2,1)}, u32[]{:S(2)}, u32[]{:S(2)}) collective-permute-start(bf16[128,1024]{0,1:T(8,128)(2,1)} %bitcast.13), channel_id=1, source_target_pairs={{0,1},{1,2},{2,3},{3,4},{4,5},{5,6},{6,7},{7,8},{8,9},{9,10},{10,1... | collective-permute-start | bytes 786440 | tf_op jit(solution)/shard_map/ppermute | solution.py:29
  111.6 22.0 %collective-permute-start.11 = (bf16[128,1024]{0,1:T(8,128)(2,1)}, bf16[128,1024]{0,1:T(8,128)(2,1)}, u32[]{:S(2)}, u32[]{:S(2)}) collective-permute-start(bf16[128,1024]{0,1:T(8,128)(2,1)} %bitcast.13), channel_id=1, source_target_pairs={{1,0},{2,1},{3,2},{4,3},{5,4},{6,5},{7,6},{8,7},{9,8},{10,9},{11,1... | collective-permute-start | bytes 786440 | tf_op jit(solution)/shard_map/ppermute | solution.py:29
  114.8 15.4 %collective-permute-start.12 = (bf16[16,1024]{0,1:T(8,128)(2,1)}, bf16[16,1024]{0,1:T(8,128)(2,1)}, u32[]{:S(2)}, u32[]{:S(2)}) collective-permute-start(bf16[16,1024]{0,1:T(8,128)(2,1)} %bitcast.16), channel_id=1, source_target_pairs={{2,0},{3,1},{4,2},{5,3},{6,4},{7,5},{8,6},{9,7},{10,8},{11,9},{12,... | collective-permute-start | bytes 98312 | tf_op jit(solution)/shard_map/ppermute | solution.py:29
  116.0 17.5 %collective-permute-start.9 = (bf16[16,1024]{0,1:T(8,128)(2,1)}, bf16[16,1024]{0,1:T(8,128)(2,1)}, u32[]{:S(2)}, u32[]{:S(2)}) collective-permute-start(bf16[16,1024]{0,1:T(8,128)(2,1)} %bitcast.14), channel_id=1, source_target_pairs={{0,2},{1,3},{2,4},{3,5},{4,6},{5,7},{6,8},{7,9},{8,10},{9,11},{10,... | collective-permute-start | bytes 98312 | tf_op jit(solution)/shard_map/ppermute | solution.py:29
  129.9 35.9 %collective-permute-start.18 = (bf16[128,512]{0,1:T(8,128)(2,1)}, bf16[128,512]{0,1:T(8,128)(2,1)}, u32[]{:S(2)}, u32[]{:S(2)}) collective-permute-start(bf16[128,512]{0,1:T(8,128)(2,1)} %get-tuple-element.97), channel_id=1, source_target_pairs={{0,1},{1,0},{2,3},{3,2},{4,5},{5,4},{6,7},{7,6},{8,9},{9,8},{10,11... | collective-permute-start | bytes 393224 | tf_op jit(solution)/shard_map/ppermute | solution.py:33
  152.9 12.8 %collective-permute-start.17 = (bf16[128,1920]{1,0:T(8,128)(2,1)}, bf16[128,1920]{1,0:T(8,128)(2,1)S(1)}, u32[]{:S(2)}, u32[]{:S(2)}) collective-permute-start(bf16[128,1920]{1,0:T(8,128)(2,1)} %get-tuple-element.48), channel_id=1, source_target_pairs={{0,1},{1,0},{2,3},{3,2},{4,5},{5,4},{6,7},{7,6},{8,9},{9,8},{10,11... | collective-permute-start | bytes 1474568 | tf_op jit(solution)/shard_map/ppermute | solution.py:33
  156.2 25.2 %all-to-all-start.2 = ((bf16[8,176,128]{2,1,0:T(8,128)(2,1)}), bf16[8,176,128]{2,1,0:T(8,128)(2,1)S(1)}, u32[]{:S(2)}, u32[]{:S(2)}) async-start(bf16[8,176,128]{2,1,0:T(8,128)(2,1)} %pad_maximum_fusion.1), calls=%async_computation.2 | async-start | bytes 720896 | tf_op jit(solution)/shard_map/all_to_all | solution.py:37
  174.0 30.9 %collective-permute-start.19 = (bf16[1920,128]{1,0:T(8,128)(2,1)}, bf16[1920,128]{1,0:T(8,128)(2,1)}, u32[]{:S(2)}, u32[]{:S(2)}) collective-permute-start(bf16[1920,128]{1,0:T(8,128)(2,1)} %convolution_convert_fusion.2), channel_id=1, source_target_pairs={{0,32},{32,64},{64,96},{96,0},{1,33},{33,65},{65,97},{97,1},{2,34}... | collective-permute-start | bytes 1474568 | tf_op jit(solution)/shard_map/ppermute | solution.py:531
  175.5 29.3 %collective-permute-start.20 = (bf16[1920,128]{1,0:T(8,128)(2,1)}, bf16[1920,128]{1,0:T(8,128)(2,1)}, u32[]{:S(2)}, u32[]{:S(2)}) collective-permute-start(bf16[1920,128]{1,0:T(8,128)(2,1)} %convolution_convert_fusion.1), channel_id=1, source_target_pairs={{0,64},{32,96},{64,0},{96,32},{1,65},{33,97},{65,1},{97,33},{2,66}... | collective-permute-start | bytes 1474568 | tf_op jit(solution)/shard_map/ppermute | solution.py:531
  178.4 26.4 %collective-permute-start.21 = (bf16[1920,128]{1,0:T(8,128)(2,1)}, bf16[1920,128]{1,0:T(8,128)(2,1)}, u32[]{:S(2)}, u32[]{:S(2)}) collective-permute-start(bf16[1920,128]{1,0:T(8,128)(2,1)} %convolution_convert_fusion), channel_id=1, source_target_pairs={{0,96},{32,0},{64,32},{96,64},{1,97},{33,1},{65,33},{97,65},{2,98}... | collective-permute-start | bytes 1474568 | tf_op jit(solution)/shard_map/ppermute | solution.py:531
  193.3 11.4 %all-to-all-start.3 = ((f32[8,48,128]{2,1,0:T(8,128)}), f32[8,48,128]{2,1,0:T(8,128)S(1)}, u32[]{:S(2)}, u32[]{:S(2)}) async-start(f32[8,48,128]{2,1,0:T(8,128)} %broadcast_in_dim.13), calls=%async_computation.3 | async-start | bytes 393216 | tf_op jit(solution)/shard_map/all_to_all | solution.py:37
  199.2 15.3 %collective-permute-start.13 = (bf16[2,2,512,256]{3,2,1,0:T(8,128)(2,1)S(1)}, bf16[2,2,512,256]{3,2,1,0:T(8,128)(2,1)}, u32[]{:S(2)}, u32[]{:S(2)}) collective-permute-start(bf16[2,2,512,256]{3,2,1,0:T(8,128)(2,1)S(1)} %get-tuple-element.53), channel_id=1, source_target_pairs={{0,1},{1,0},{2,3},{3,2},{4,5},{5,4},{6,7},{7,6},{8,9},{9,8},{10,11... | collective-permute-start | bytes 3145736 | tf_op jit(solution)/shard_map/ppermute | solution.py:33
  204.7 7.4 %collective-permute-start.15 = (f32[48,128]{1,0:T(8,128)S(1)}, f32[48,128]{1,0:T(8,128)S(1)}, u32[]{:S(2)}, u32[]{:S(2)}) collective-permute-start(f32[48,128]{1,0:T(8,128)S(1)} %reduce_sum.48), channel_id=1, source_target_pairs={{0,1},{1,0},{2,3},{3,2},{4,5},{5,4},{6,7},{7,6},{8,9},{9,8},{10,11... | collective-permute-start | bytes 73736 | tf_op jit(solution)/shard_map/ppermute | solution.py:33
  208.6 7.8 %collective-permute-start.22 = (bf16[16,60,128]{2,1,0:T(8,128)(2,1)S(1)}, bf16[16,60,128]{2,1,0:T(8,128)(2,1)S(1)}, u32[]{:S(2)}, u32[]{:S(2)}) collective-permute-start(bf16[16,60,128]{2,1,0:T(8,128)(2,1)S(1)} %fusion.20), channel_id=1, source_target_pairs={{0,0},{1,128},{128,1},{129,129},{2,2},{3,130},{130,3},{131,131},{4... | collective-permute-start | bytes 737288 | tf_op jit(solution)/shard_map/ppermute | solution.py:543
  212.0 6.7 %collective-permute-start.23 = (bf16[16,60,128]{2,1,0:T(8,128)(2,1)S(1)}, bf16[16,60,128]{2,1,0:T(8,128)(2,1)S(1)}, u32[]{:S(2)}, u32[]{:S(2)}) collective-permute-start(bf16[16,60,128]{2,1,0:T(8,128)(2,1)S(1)} %fusion.19), channel_id=1, source_target_pairs={{0,1},{1,129},{128,0},{129,128},{2,3},{3,131},{130,2},{131,130},{4... | collective-permute-start | bytes 737288 | tf_op jit(solution)/shard_map/ppermute | solution.py:543
  212.2 4.2 %collective-permute-start.16 = (f32[48,128]{1,0:T(8,128)S(1)}, f32[48,128]{1,0:T(8,128)S(1)}, u32[]{:S(2)}, u32[]{:S(2)}) collective-permute-start(f32[48,128]{1,0:T(8,128)S(1)} %add.104), channel_id=1, source_target_pairs={{0,8},{8,0},{1,9},{9,1},{2,10},{10,2},{3,11},{11,3},{4,12},{12,4},... | collective-permute-start | bytes 73736 | tf_op jit(solution)/shard_map/ppermute | solution.py:33
  216.0 14.1 %collective-permute-start.14 = (bf16[2,512,256]{2,1,0:T(8,128)(2,1)S(1)}, bf16[2,512,256]{2,1,0:T(8,128)(2,1)S(1)}, u32[]{:S(2)}, u32[]{:S(2)}) collective-permute-start(bf16[2,512,256]{2,1,0:T(8,128)(2,1)S(1)} %fusion.18), channel_id=1, source_target_pairs={{0,8},{8,0},{1,9},{9,1},{2,10},{10,2},{3,11},{11,3},{4,12},{12,4},... | collective-permute-start | bytes 1572872 | tf_op jit(solution)/shard_map/ppermute | solution.py:33
  230.1 5.1 %collective-permute-start.24 = (bf16[2,4,60,128]{3,2,1,0:T(8,128)(2,1)S(1)}, bf16[2,4,60,128]{3,2,1,0:T(8,128)(2,1)S(1)}, u32[]{:S(2)}, u32[]{:S(2)}) collective-permute-start(bf16[2,4,60,128]{3,2,1,0:T(8,128)(2,1)S(1)} %fusion.22), channel_id=1, source_target_pairs={{0,8},{8,0},{1,9},{9,1},{2,10},{10,2},{3,11},{11,3},{4,12},{12,4},... | collective-permute-start | bytes 368648 | tf_op jit(solution)/shard_map/ppermute | solution.py:33
  (18 other events, 212.0 us)

commit v3 on v2

--- a/solution.py
+++ b/solution.py
@@ -471,11 +471,13 @@
 
 
 def both_sides(rows):
-    return (
-        from_behind(rows[-FAR:], 2),
-        from_behind(rows, 1),
-        from_behind(rows, -1),
-        from_behind(rows[:FAR], -2),
+    return jnp.concatenate(
+        [
+            from_behind(rows[-FAR:], 2),
+            from_behind(rows, 1),
+            from_behind(rows, -1),
+            from_behind(rows[:FAR], -2),
+        ]
     )
 
 
@@ -523,34 +525,51 @@
     return lax.optimization_barrier(pieces)
 
 
-def weight_over_y(pieces):
+def over_y(pieces):
     peers = len(pieces)
     total = pieces[0].astype(jnp.float32)
     for step in range(1, peers):
         pairs = [(i, (i + step) % peers) for i in range(peers)]
         total = total + lax.ppermute(pieces[step], "y", pairs).astype(jnp.float32)
-    return total.astype(jnp.bfloat16)
-
-
-def weight_over_zl(total):
+    return total
+
+
+def all_over_y(part):
+    peers = lax.axis_size("y")
+    parts = [part]
+    for step in range(1, peers):
+        pairs = [(i, (i + step) % peers) for i in range(peers)]
+        parts.append(lax.ppermute(part, "y", pairs))
+    while len(parts) > 1:
+        half = len(parts) // 2
+        parts = [parts[i] + parts[i + half] for i in range(half)]
+    return parts[0]
+
+
+def over_zl_and_xb(total, small):
     zl = lax.axis_index("zl")
-    total = total.reshape(16, 2, D // 32, -1)
-    halves = (total[:, 0], total[:, 1])
-    received = []
+    xb = lax.axis_index("xb")
+    total = total.astype(jnp.bfloat16).reshape(2, 2, 4, 2, D // 32, -1)
+    width = total.shape[-1]
+    small = small.astype(jnp.bfloat16).reshape(1, -1, width)
+    total = jnp.where(xb == 0, total, total[:, ::-1])
+    total = jnp.where(zl == 0, total, total[:, :, :, ::-1])
+    received = None
     for turn in range(2):
-        piece = jnp.where(zl == 0, halves[turn], halves[1 - turn])
-        pairs = [(a * 2 + b, b * 2 + (a ^ turn)) for a in range(2) for b in range(2)]
-        received.append(lax.ppermute(piece, ("zl", "c"), pairs).astype(jnp.float32))
-    return (received[0] + received[1]).astype(jnp.bfloat16)
-
-
-def weight_over_xb(total):
-    xb = lax.axis_index("xb")
-    total = total.reshape(2, 2, 4, D // 32, -1)
-    mine = jnp.where(xb == 0, total[:, 0], total[:, 1]).astype(jnp.float32)
-    theirs = jnp.where(xb == 0, total[:, 1], total[:, 0])
-    total = mine + swap(theirs, "xb").astype(jnp.float32)
-    return total.astype(jnp.bfloat16).reshape(8, D // 32, -1)
+        for move in range(2):
+            piece = total[:, move, :, turn].reshape(1, -1, width)
+            piece = jnp.concatenate([piece, small], axis=1)[0]
+            pairs = [
+                (a * 4 + x * 2 + b, b * 4 + (x ^ move) * 2 + (a ^ turn))
+                for a in range(2)
+                for x in range(2)
+                for b in range(2)
+            ]
+            part = lax.ppermute(piece, ("zl", "xb", "c"), pairs).astype(jnp.float32)
+            received = [part] if received is None else received + [part]
+    total = (received[0] + received[1]) + (received[2] + received[3])
+    rows = 8 * (D // 32)
+    return total[:rows].astype(jnp.bfloat16).reshape(8, D // 32, width), total[rows:]
 
 
 def local(
@@ -573,19 +592,14 @@
     qkv_own = exchange(qkv_send, HEAD_AXES)
     query_rows = qkv_own[:, :tok_rows].reshape(8 * tok_rows, HDIM)
     kv_all = gather_keys(qkv_own[:, tok_rows:])
-    apart = lax.optimization_barrier((residual[0], cotangent[0], qkv_own))
-    res_sides = both_sides(apart[0])
-    cot_sides = (from_behind(apart[1], -1), from_behind(apart[1][:FAR], -2))
+    cot_sides = (from_behind(cotangent[0], -1), from_behind(cotangent[0, :FAR], -2))
     query_total = 8 * tok_rows
     place = jnp.stack([lax.axis_index("xb"), lax.axis_index("c")]).astype(jnp.int32)
     head_out, log_total = attend(place, query_rows, kv_all)
-    head_out, res_sides, cot_sides = lax.optimization_barrier((head_out, res_sides, cot_sides))
+    head_out, cot_sides = lax.optimization_barrier((head_out, cot_sides))
     attention = from_heads(exchange(head_out.reshape(8, tok_rows, HDIM), HEAD_AXES))
-    att_sides = both_sides(attention)
     x_first, inv_rms, normed = first_norm(residual[0], attention, w_out, norm_gain)
-    _, _, sides = first_norm(
-        jnp.concatenate(res_sides), jnp.concatenate(att_sides), w_out, norm_gain
-    )
+    sides = both_sides(normed)
     layer_out, grad_residual, small = hyena(
         normed,
         sides,
@@ -607,33 +621,26 @@
     grad_recv = exchange(
         jnp.concatenate([to_heads(grad_attention), small_send], axis=1), HEAD_AXES
     )
-    weight_part = weight_over_y(weight_pieces(attention, grad_residual))
+    pieces = weight_pieces(attention, grad_residual)
+    weight_part = over_y(pieces)
     grad_rows_all = grad_recv[:, :tok_rows].reshape(query_total, HDIM)
     small_part = jnp.sum(grad_recv[:, tok_rows:].astype(jnp.float32), axis=0)
     grad_query, same_core, other_core = attend_back(
         place, query_rows, kv_all, head_out, log_total, grad_rows_all
     )
-    dq_send = grad_query.reshape(8, tok_rows, HDIM)
+    small_part, _ = lax.optimization_barrier((small_part, grad_query))
+    small_part = all_over_y(small_part + swap(small_part, "c"))
+    grad_query = exchange(grad_query.reshape(8, tok_rows, HDIM), HEAD_AXES)
     dkv = same_core.astype(jnp.float32) + swap(other_core, "c").astype(jnp.float32)
     dkv_far = swap(dkv[:, 1].astype(jnp.bfloat16), "xb")
-    small_part, _ = lax.optimization_barrier((small_part, grad_query))
-    sequences = lax.axis_size(DP_AXES)
-    small_part = exchange(
-        jnp.broadcast_to(small_part[None], (sequences,) + small_part.shape), DP_AXES
-    )
-    small_part = jnp.sum(small_part, axis=0)
-    small_part = small_part + swap(small_part, "c")
-    small_part = small_part + swap(small_part, "xb")
-    small_part = small_part.astype(jnp.bfloat16)
-    weight_part = weight_over_zl(weight_part)
-    weight_part, _ = lax.optimization_barrier((weight_part, dkv_far))
     dkv = dkv[:, 0] + dkv_far.astype(jnp.float32)
     dkv = dkv.reshape(8, tok_rows, 2 * HDIM).astype(jnp.bfloat16)
-    weight_part = weight_over_xb(weight_part)
+    weight_part, _ = lax.optimization_barrier((weight_part, grad_query))
+    weight_part, small_part = over_zl_and_xb(weight_part, small_part)
+    small_part = small_part.reshape(-1, HDIM).astype(jnp.bfloat16)
     weight_rows = weight_part.size // (8 * HDIM)
     last_send = jnp.concatenate(
         [
-            dq_send,
             dkv[:, :, :HDIM],
             dkv[:, :, HDIM:],
             jnp.broadcast_to(small_part[None], (8,) + small_part.shape),
@@ -642,10 +649,10 @@
         axis=1,
     )
     last = exchange(last_send, HEAD_AXES)
-    grad_query = from_heads(last[:, :tok_rows])
-    grad_key = from_heads(last[:, tok_rows : 2 * tok_rows])
-    grad_value = from_heads(last[:, 2 * tok_rows : 3 * tok_rows])
-    sums_back = last[:, 3 * tok_rows :].astype(jnp.float32)
+    grad_query = from_heads(grad_query)
+    grad_key = from_heads(last[:, :tok_rows])
+    grad_value = from_heads(last[:, tok_rows : 2 * tok_rows])
+    sums_back = last[:, 2 * tok_rows :].astype(jnp.float32)
     small_back = sums_back[:, :small_rows]
     small_back = small_back.reshape(FILTERS + 1, SMALL, FCH)[:FILTERS].transpose(1, 0, 2)
     grad_filters = small_back[SMALL - 1]

time: 278 us -> 250 us (0.90)
  the two profiles are of different devices: /device:TPU:32 before, /device:TPU:1 now
where the time goes in v3:
time: 250 us; the launch traced here: 249 us
  starting transfers between devices  83.6 us (33%)
  waiting for transfers between devices  61.3 us (25%)
  blocking collectives  32.7 us (13%)
  Pallas kernels  28.2 us (11%)
  local copies, waits for them, and re-layouts  16.4 us (7%)
  matrix products  13.6 us (5%)
  other arithmetic  11.6 us (5%)
    all_to_all x4, starting transfers between devices, exchange(): return lax.all_to_all(x, axes, split_axis=0, concat_axis=0, tiled=True)  35.3 us
    all_to_all x4, waiting for transfers between devices, exchange(): return lax.all_to_all(x, axes, split_axis=0, concat_axis=0, tiled=True)  35.3 us
    all_to_all x1, blocking collectives, exchange(): return lax.all_to_all(x, axes, split_axis=0, concat_axis=0, tiled=True)  32.7 us
    ppermute x6, starting transfers between devices, from_behind(): return lax.ppermute(x, CTX_AXES, pairs)  18.8 us
    pallas_call x1, Pallas kernels, hyena(): pl.pallas_call(hyena_kernel, grid=(FILTERS,), in_specs=[part(rows), part(...  13.9 us
    ppermute x4, starting transfers between devices, over_zl_and_xb(): part = lax.ppermute(piece, ('zl', 'xb', 'c'), pairs).astype(jnp.float32)  10.4 us
    ppermute x8, starting transfers between devices, swap(): return lax.ppermute(x, axis, [(0, 1), (1, 0)])  9.69 us
    ppermute x4, waiting for transfers between devices, over_zl_and_xb(): part = lax.ppermute(piece, ('zl', 'xb', 'c'), pairs).astype(jnp.float32)  8.76 us
  transfers between devices with their start and end apart: 28, of which 10 were waited for; matrix products, arithmetic and copies ran while one was open for 9% of the time, Pallas kernels for 11%

profile of v3, /device:TPU:1, one launch (start us, length us, event | category | flops | bytes accessed | tf_op | source)
XLA Modules:
  0.0 248.8 jit_solution(8077467456602951244)
XLA Ops:
  3.8 32.7 %all_to_all.25 = bf16[8,384,128]{2,1,0:T(8,128)(2,1)S(1)} all-to-all(bf16[8,384,128]{2,1,0:T(8,128)(2,1)S(1)} %pad_maximum_fusion.1), channel_id=1, replica_groups=mesh['zl'=2,'y'=4,'xa'=2,'xb'=2,'zh'=4,'c'=2] {'xa','zh'}, dimensions={0} | all-to-all | bytes 1572864 | tf_op jit(solution)/shard_map/all_to_all | solution.py:37
  36.9 4.9 %collective-permute-start.3 = (bf16[128,1920]{1,0:T(8,128)(2,1)S(1)}, bf16[128,1920]{1,0:T(8,128)(2,1)S(1)}, u32[]{:S(2)}, u32[]{:S(2)}) collective-permute-start(bf16[128,1920]{1,0:T(8,128)(2,1)S(1)} %bitcast.82), channel_id=1, source_target_pairs={{1,0},{2,1},{3,2},{4,3},{5,4},{6,5},{7,6},{8,7},{9,8},{10,9},{11,1... | collective-permute-start | bytes 1474568 | tf_op jit(solution)/shard_map/ppermute | solution.py:29
  42.0 5.3 %collective-permute-done.far = bf16[8,256,128]{2,1,0:T(8,128)(2,1)S(1)} collective-permute-done((bf16[8,256,128]{2,1,0:T(8,128)(2,1)S(1)}, bf16[8,256,128]{2,1,0:T(8,128)(2,1)S(1)}, u32[]{:S(2)}, u32[]{:S(2)}) %collective-permute-start) | collective-permute-done | bytes 524320 | tf_op jit(solution)/shard_map/ppermute | solution.py:33
  47.3 3.7 %collective-permute-start.2 = (bf16[8,256,128]{2,1,0:T(8,128)(2,1)S(1)}, bf16[8,256,128]{2,1,0:T(8,128)(2,1)}, u32[]{:S(2)}, u32[]{:S(2)}) collective-permute-start(bf16[8,256,128]{2,1,0:T(8,128)(2,1)S(1)} %collective-permute-done.far), channel_id=1, source_target_pairs={{0,1},{1,0},{2,3},{3,2},{4,5},{5,4},{6,7},{7,6},{8,9},{9,8},{10,11... | collective-permute-start | bytes 1572872 | tf_op jit(solution)/shard_map/ppermute | solution.py:33
  53.4 5.7 %shard_map.177 = (bf16[1024,128]{1,0:T(8,128)(2,1)S(1)}, f32[1,1024]{1,0:T(1,128)S(1)}) custom-call(s32[2]{0:T(128)S(1)} %pad_add_fusion.place, bf16[1024,128]{1,0:T(8,128)(2,1)S(1)} %bitcast.84, bf16[8,256,128]{2,1,0:T(8,128)(2,1)S(1)} %slice.129.own, bf16[8,256,128]{2,1,0:T(8,128)(2,1)S(1)} %collective-permute-done.far, ...), custom_call_target="tpu_custom_call" | custom-call | flops 1600000000 | bytes 3000000 | tf_op jit(solution)/shard_map/pallas_call | solution.py:362
  60.1 9.3 %all-to-all-start.1 = ((bf16[8,128,128]{1,2,0:T(8,128)(2,1)}), bf16[8,128,128]{1,2,0:T(8,128)(2,1)S(1)}, u32[]{:S(2)}, u32[]{:S(2)}) async-start(bf16[8,128,128]{1,2,0:T(8,128)(2,1)} %copy.62), calls=%async_computation.1 | async-start | bytes 524288 | tf_op jit(solution)/shard_map/all_to_all | solution.py:37
  71.3 8.0 %all-to-all-done.1 = bf16[8,128,128]{1,2,0:T(8,128)(2,1)S(1)} async-done(((bf16[8,128,128]{1,2,0:T(8,128)(2,1)}), bf16[8,128,128]{1,2,0:T(8,128)(2,1)S(1)}, u32[]{:S(2)}, u32[]{:S(2)}) %all-to-all-start.1) | async-done | bytes 262176 | tf_op jit(solution)/shard_map/all_to_all | solution.py:37
  79.3 3.1 %fusion.x_all = bf16[128,1920]{1,0:T(8,128)(2,1)S(1)} fusion(bf16[128,1024]{0,1:T(8,128)(2,1)S(1)} %bitcast.88, bf16[1024,1920]{1,0:T(8,128)(2,1)} %param.14, bf16[1,128,1920]{2,1,0:T(8,128)(2,1)} %param.13), kind=kOutput, calls=%fused_computation.1 | convolution fusion | flops 504053760 | bytes 5177344 | tf_op jit(solution)/shard_map/dot_general | solution.py:485
  82.7 4.8 %collective-permute-start.6 = (bf16[128,1920]{1,0:T(8,128)(2,1)S(1)}, bf16[128,1920]{1,0:T(8,128)(2,1)}, u32[]{:S(2)}, u32[]{:S(2)}) collective-permute-start(bf16[128,1920]{1,0:T(8,128)(2,1)S(1)} %fusion.6.own), channel_id=1, source_target_pairs={{0,1},{1,2},{2,3},{3,4},{4,5},{5,6},{6,7},{7,8},{8,9},{9,10},{10,1... | collective-permute-start | bytes 1474568 | tf_op jit(solution)/shard_map/ppermute | solution.py:29
  87.5 2.7 %collective-permute-start.7 = (bf16[128,1920]{1,0:T(8,128)(2,1)S(1)}, bf16[128,1920]{1,0:T(8,128)(2,1)}, u32[]{:S(2)}, u32[]{:S(2)}) collective-permute-start(bf16[128,1920]{1,0:T(8,128)(2,1)S(1)} %fusion.6.own), channel_id=1, source_target_pairs={{1,0},{2,1},{3,2},{4,3},{5,4},{6,5},{7,6},{8,7},{9,8},{10,9},{11,1... | collective-permute-start | bytes 1474568 | tf_op jit(solution)/shard_map/ppermute | solution.py:29
  90.9 3.8 %collective-permute-start.5 = (bf16[16,1920]{1,0:T(8,128)(2,1)}, bf16[16,1920]{1,0:T(8,128)(2,1)}, u32[]{:S(2)}, u32[]{:S(2)}) collective-permute-start(bf16[16,1920]{1,0:T(8,128)(2,1)} %get-tuple-element.78), channel_id=1, source_target_pairs={{0,2},{1,3},{2,4},{3,5},{4,6},{5,7},{6,8},{7,9},{8,10},{9,11},{10,... | collective-permute-start | bytes 184328 | tf_op jit(solution)/shard_map/ppermute | solution.py:29
  99.0 6.5 %collective-permute-done.8 = bf16[16,1920]{1,0:T(8,128)(2,1)} collective-permute-done((bf16[16,1920]{1,0:T(8,128)(2,1)}, bf16[16,1920]{1,0:T(8,128)(2,1)}, u32[]{:S(2)}, u32[]{:S(2)}) %collective-permute-start.8) | collective-permute-done | bytes 61472 | tf_op jit(solution)/shard_map/ppermute | solution.py:29
  106.8 13.9 %shard_map.179 = (bf16[128,1920]{1,0:T(8,128)(2,1)}, bf16[128,1920]{1,0:T(8,128)(2,1)}, f32[16,24,128]{2,1,0:T(8,128)S(1)}) custom-call(bf16[128,1920]{1,0:T(8,128)(2,1)S(1)} %fusion.6.own, bf16[288,1920]{1,0:T(8,128)(2,1)S(1)} %pad_maximum_fusion.sides, bf16[128,1920]{1,0:T(8,128)(2,1)S(1)} %fusion.x_all, bf16[128,1920]{1,0:T(8,128)(2,1)S(1)} %bitcast.83, ...), custom_call_target="tpu_custom_call" | custom-call | flops 503316480 | bytes 12582912 | tf_op jit(solution)/shard_map/pallas_call | solution.py:227
  121.3 2.4 fusion.1
  124.6 13.6 %all-to-all-start.2 = ((bf16[8,176,128]{2,1,0:T(8,128)(2,1)}), bf16[8,176,128]{2,1,0:T(8,128)(2,1)S(1)}, u32[]{:S(2)}, u32[]{:S(2)}) async-start(bf16[8,176,128]{2,1,0:T(8,128)(2,1)} %pad_maximum_fusion.3), calls=%async_computation.2 | async-start | bytes 720896 | tf_op jit(solution)/shard_map/all_to_all | solution.py:37
  138.3 2.0 convolution_convert_fusion
  140.3 2.0 convolution_convert_fusion.1
  142.3 2.1 convolution_convert_fusion.2
  144.4 2.0 convolution_convert_fusion.3
  147.8 2.6 %collective-permute-start.14 = (bf16[1920,128]{1,0:T(8,128)(2,1)}, bf16[1920,128]{1,0:T(8,128)(2,1)}, u32[]{:S(2)}, u32[]{:S(2)}) collective-permute-start(bf16[1920,128]{1,0:T(8,128)(2,1)} %convolution_convert_fusion.1), channel_id=1, source_target_pairs={{0,64},{32,96},{64,0},{96,32},{1,65},{33,97},{65,1},{97,33},{2,66}... | collective-permute-start | bytes 1474568 | tf_op jit(solution)/shard_map/ppermute | solution.py:533
  154.3 8.0 %shard_map.180 = (bf16[1024,128]{1,0:T(8,128)(2,1)}, bf16[2,2,512,256]{3,2,1,0:T(8,128)(2,1)S(1)}, bf16[2,2,512,256]{3,2,1,0:T(8,128)(2,1)S(1)}) custom-call(s32[2]{0:T(128)S(1)} %pad_add_fusion.place, bf16[1024,128]{1,0:T(8,128)(2,1)S(1)} %bitcast.85, bf16[8,256,128]{2,1,0:T(8,128)(2,1)S(1)} %copy-done.3, bf16[8,256,128]{2,1,0:T(8,128)(2,1)S(1)} %copy-done.9, ...), custom_call_target="tpu_custom_call" | custom-call | flops 4000000000 | bytes 6000000 | tf_op jit(solution)/shard_map/pallas_call | solution.py:458
  165.2 2.7 %collective-permute-start.17 = (f32[48,128]{1,0:T(8,128)S(1)}, f32[48,128]{1,0:T(8,128)S(1)}, u32[]{:S(2)}, u32[]{:S(2)}) collective-permute-start(f32[48,128]{1,0:T(8,128)S(1)} %add.110), channel_id=1, source_target_pairs={{0,64},{32,96},{64,0},{96,32},{1,65},{33,97},{65,1},{97,33},{2,66}... | collective-permute-start | bytes 73736 | tf_op jit(solution)/shard_map/ppermute | solution.py:542
  168.3 4.5 %collective-permute-done.17 = f32[48,128]{1,0:T(8,128)S(1)} collective-permute-done((f32[48,128]{1,0:T(8,128)S(1)}, f32[48,128]{1,0:T(8,128)S(1)}, u32[]{:S(2)}, u32[]{:S(2)}) %collective-permute-start.17) | collective-permute-done | bytes 24608 | tf_op jit(solution)/shard_map/ppermute | solution.py:542
  174.0 8.7 %all-to-all-start.3 = ((bf16[8,128,128]{2,1,0:T(8,128)(2,1)}), bf16[8,128,128]{2,1,0:T(8,128)(2,1)}, u32[]{:S(2)}, u32[]{:S(2)}) async-start(bf16[8,128,128]{2,1,0:T(8,128)(2,1)} %bitcast.21), calls=%async_computation.3 | async-start | bytes 524288 | tf_op jit(solution)/shard_map/all_to_all | solution.py:37
  182.7 2.6 %collective-permute-start.9 = (bf16[2,2,512,256]{3,2,1,0:T(8,128)(2,1)S(1)}, bf16[2,2,512,256]{3,2,1,0:T(8,128)(2,1)}, u32[]{:S(2)}, u32[]{:S(2)}) collective-permute-start(bf16[2,2,512,256]{3,2,1,0:T(8,128)(2,1)S(1)} %get-tuple-element.41), channel_id=1, source_target_pairs={{0,1},{1,0},{2,3},{3,2},{4,5},{5,4},{6,7},{7,6},{8,9},{9,8},{10,11... | collective-permute-start | bytes 3145736 | tf_op jit(solution)/shard_map/ppermute | solution.py:33
  185.4 1.7 convert_add_fusion.1
  187.1 5.8 %all-to-all-done.3 = bf16[8,128,128]{2,1,0:T(8,128)(2,1)} async-done(((bf16[8,128,128]{2,1,0:T(8,128)(2,1)}), bf16[8,128,128]{2,1,0:T(8,128)(2,1)}, u32[]{:S(2)}, u32[]{:S(2)}) %all-to-all-start.3) | async-done | bytes 262176 | tf_op jit(solution)/shard_map/all_to_all | solution.py:37
  195.1 7.6 %collective-permute-start.20 = (bf16[528,128]{1,0:T(8,128)(2,1)S(1)}, bf16[528,128]{1,0:T(8,128)(2,1)S(1)}, u32[]{:S(2)}, u32[]{:S(2)}) collective-permute-start(bf16[528,128]{1,0:T(8,128)(2,1)S(1)} %get-tuple-element.83), channel_id=1, source_target_pairs={{0,0},{1,128},{8,8},{9,136},{128,1},{129,129},{136,9},{137,137},{2... | collective-permute-start | bytes 405512 | tf_op jit(solution)/shard_map/ppermute | solution.py:568
  205.8 2.6 %collective-permute-done.21 = bf16[528,128]{1,0:T(8,128)(2,1)S(1)} collective-permute-done((bf16[528,128]{1,0:T(8,128)(2,1)S(1)}, bf16[528,128]{1,0:T(8,128)(2,1)S(1)}, u32[]{:S(2)}, u32[]{:S(2)}) %collective-permute-start.21) | collective-permute-done | bytes 135200 | tf_op jit(solution)/shard_map/ppermute | solution.py:568
  208.4 5.9 %collective-permute-done.23 = bf16[528,128]{1,0:T(8,128)(2,1)S(1)} collective-permute-done((bf16[528,128]{1,0:T(8,128)(2,1)S(1)}, bf16[528,128]{1,0:T(8,128)(2,1)S(1)}, u32[]{:S(2)}, u32[]{:S(2)}) %collective-permute-start.23) | collective-permute-done | bytes 135200 | tf_op jit(solution)/shard_map/ppermute | solution.py:568
  216.8 3.7 %all-to-all-start.4 = ((bf16[8,364,128]{2,1,0:T(8,128)(2,1)}), bf16[8,364,128]{2,1,0:T(8,128)(2,1)S(1)}, u32[]{:S(2)}, u32[]{:S(2)}) async-start(bf16[8,364,128]{2,1,0:T(8,128)(2,1)} %pad_maximum_fusion.2), calls=%async_computation.4 | async-start | bytes 1507328 | tf_op jit(solution)/shard_map/all_to_all | solution.py:37
  222.4 21.6 %all-to-all-done.4 = bf16[8,364,128]{2,1,0:T(8,128)(2,1)S(1)} async-done(((bf16[8,364,128]{2,1,0:T(8,128)(2,1)}), bf16[8,364,128]{2,1,0:T(8,128)(2,1)S(1)}, u32[]{:S(2)}, u32[]{:S(2)}) %all-to-all-start.4) | async-done | bytes 745504 | tf_op jit(solution)/shard_map/all_to_all | solution.py:37
  (151 shorter events, 40.8 us)
Async XLA Ops:
  3.7 33.2 %copy-start = (bf16[1,128,1920]{2,1,0:T(8,128)(2,1)S(1)}, bf16[1,128,1920]{2,1,0:T(8,128)(2,1)}, u32[]{:S(2)}) copy-start(bf16[1,128,1920]{2,1,0:T(8,128)(2,1)} %param.19) | copy-start | bytes 1474564
  36.5 22.6 %copy-start.2 = (bf16[8,256,128]{2,1,0:T(8,128)(2,1)}, bf16[8,256,128]{2,1,0:T(8,128)(2,1)S(1)}, u32[]{:S(2)}) copy-start(bf16[8,256,128]{2,1,0:T(8,128)(2,1)S(1)} %slice.129.own) | copy-start | bytes 1572868
  36.5 10.8 %collective-permute-start = (bf16[8,256,128]{2,1,0:T(8,128)(2,1)S(1)}, bf16[8,256,128]{2,1,0:T(8,128)(2,1)S(1)}, u32[]{:S(2)}, u32[]{:S(2)}) collective-permute-start(bf16[8,256,128]{2,1,0:T(8,128)(2,1)S(1)} %slice.129.own), channel_id=1, source_target_pairs={{0,8},{8,0},{1,9},{9,1},{2,10},{10,2},{3,11},{11,3},{4,12},{12,4},... | collective-permute-start | bytes 1572872 | tf_op jit(solution)/shard_map/ppermute | solution.py:33
  36.9 22.2 %collective-permute-start.3 = (bf16[128,1920]{1,0:T(8,128)(2,1)S(1)}, bf16[128,1920]{1,0:T(8,128)(2,1)S(1)}, u32[]{:S(2)}, u32[]{:S(2)}) collective-permute-start(bf16[128,1920]{1,0:T(8,128)(2,1)S(1)} %bitcast.82), channel_id=1, source_target_pairs={{1,0},{2,1},{3,2},{4,3},{5,4},{6,5},{7,6},{8,7},{9,8},{10,9},{11,1... | collective-permute-start | bytes 1474568 | tf_op jit(solution)/shard_map/ppermute | solution.py:29
  41.9 11.5 %collective-permute-start.1 = (bf16[8,256,128]{2,1,0:T(8,128)(2,1)S(1)}, bf16[8,256,128]{2,1,0:T(8,128)(2,1)S(1)}, u32[]{:S(2)}, u32[]{:S(2)}) collective-permute-start(bf16[8,256,128]{2,1,0:T(8,128)(2,1)S(1)} %slice.129.own), channel_id=1, source_target_pairs={{0,1},{1,0},{2,3},{3,2},{4,5},{5,4},{6,7},{7,6},{8,9},{9,8},{10,11... | collective-permute-start | bytes 1572872 | tf_op jit(solution)/shard_map/ppermute | solution.py:33
  47.3 6.0 %collective-permute-start.2 = (bf16[8,256,128]{2,1,0:T(8,128)(2,1)S(1)}, bf16[8,256,128]{2,1,0:T(8,128)(2,1)}, u32[]{:S(2)}, u32[]{:S(2)}) collective-permute-start(bf16[8,256,128]{2,1,0:T(8,128)(2,1)S(1)} %collective-permute-done.far), channel_id=1, source_target_pairs={{0,1},{1,0},{2,3},{3,2},{4,5},{5,4},{6,7},{7,6},{8,9},{9,8},{10,11... | collective-permute-start | bytes 1572872 | tf_op jit(solution)/shard_map/ppermute | solution.py:33
  51.0 8.2 %collective-permute-start.4 = (bf16[16,1920]{1,0:T(8,128)(2,1)S(1)}, bf16[16,1920]{1,0:T(8,128)(2,1)S(1)}, u32[]{:S(2)}, u32[]{:S(2)}) collective-permute-start(bf16[16,1920]{1,0:T(8,128)(2,1)S(1)} %slice_bitcast_fusion.2), channel_id=1, source_target_pairs={{2,0},{3,1},{4,2},{5,3},{6,4},{7,5},{8,6},{9,7},{10,8},{11,9},{12,... | collective-permute-start | bytes 184328 | tf_op jit(solution)/shard_map/ppermute | solution.py:29
  53.4 17.2 %copy-start.19 = (f32[1920]{0:T(1024)S(1)}, f32[1920]{0:T(1024)}, u32[]{:S(2)}) copy-start(f32[1920]{0:T(1024)} %param.15) | copy-start | bytes 23044
  53.4 17.2 %copy-start.21 = (f32[1920]{0:T(1024)S(1)}, f32[1920]{0:T(1024)}, u32[]{:S(2)}) copy-start(f32[1920]{0:T(1024)} %param.18) | copy-start | bytes 23044
  60.1 19.2 %all-to-all-start.1 = ((bf16[8,128,128]{1,2,0:T(8,128)(2,1)}), bf16[8,128,128]{1,2,0:T(8,128)(2,1)S(1)}, u32[]{:S(2)}, u32[]{:S(2)}) async-start(bf16[8,128,128]{1,2,0:T(8,128)(2,1)} %copy.62), calls=%async_computation.1 | async-start | bytes 524288 | tf_op jit(solution)/shard_map/all_to_all | solution.py:37
  82.7 22.8 %collective-permute-start.6 = (bf16[128,1920]{1,0:T(8,128)(2,1)S(1)}, bf16[128,1920]{1,0:T(8,128)(2,1)}, u32[]{:S(2)}, u32[]{:S(2)}) collective-permute-start(bf16[128,1920]{1,0:T(8,128)(2,1)S(1)} %fusion.6.own), channel_id=1, source_target_pairs={{0,1},{1,2},{2,3},{3,4},{4,5},{5,6},{6,7},{7,8},{8,9},{9,10},{10,1... | collective-permute-start | bytes 1474568 | tf_op jit(solution)/shard_map/ppermute | solution.py:29
  87.5 18.0 %collective-permute-start.7 = (bf16[128,1920]{1,0:T(8,128)(2,1)S(1)}, bf16[128,1920]{1,0:T(8,128)(2,1)}, u32[]{:S(2)}, u32[]{:S(2)}) collective-permute-start(bf16[128,1920]{1,0:T(8,128)(2,1)S(1)} %fusion.6.own), channel_id=1, source_target_pairs={{1,0},{2,1},{3,2},{4,3},{5,4},{6,5},{7,6},{8,7},{9,8},{10,9},{11,1... | collective-permute-start | bytes 1474568 | tf_op jit(solution)/shard_map/ppermute | solution.py:29
  90.9 8.1 %collective-permute-start.5 = (bf16[16,1920]{1,0:T(8,128)(2,1)}, bf16[16,1920]{1,0:T(8,128)(2,1)}, u32[]{:S(2)}, u32[]{:S(2)}) collective-permute-start(bf16[16,1920]{1,0:T(8,128)(2,1)} %get-tuple-element.78), channel_id=1, source_target_pairs={{0,2},{1,3},{2,4},{3,5},{4,6},{5,7},{6,8},{7,9},{8,10},{9,11},{10,... | collective-permute-start | bytes 184328 | tf_op jit(solution)/shard_map/ppermute | solution.py:29
  94.7 10.8 %collective-permute-start.8 = (bf16[16,1920]{1,0:T(8,128)(2,1)}, bf16[16,1920]{1,0:T(8,128)(2,1)}, u32[]{:S(2)}, u32[]{:S(2)}) collective-permute-start(bf16[16,1920]{1,0:T(8,128)(2,1)} %get-tuple-element.79), channel_id=1, source_target_pairs={{2,0},{3,1},{4,2},{5,3},{6,4},{7,5},{8,6},{9,7},{10,8},{11,9},{12,... | collective-permute-start | bytes 184328 | tf_op jit(solution)/shard_map/ppermute | solution.py:29
  97.8 40.4 %collective-permute-start.12 = (bf16[128,512]{0,1:T(8,128)(2,1)}, bf16[128,512]{0,1:T(8,128)(2,1)}, u32[]{:S(2)}, u32[]{:S(2)}) collective-permute-start(bf16[128,512]{0,1:T(8,128)(2,1)} %get-tuple-element.80), channel_id=1, source_target_pairs={{0,1},{1,0},{2,3},{3,2},{4,5},{5,4},{6,7},{7,6},{8,9},{9,8},{10,11... | collective-permute-start | bytes 393224 | tf_op jit(solution)/shard_map/ppermute | solution.py:33
  120.8 17.4 %collective-permute-start.11 = (bf16[128,1920]{1,0:T(8,128)(2,1)}, bf16[128,1920]{1,0:T(8,128)(2,1)S(1)}, u32[]{:S(2)}, u32[]{:S(2)}) collective-permute-start(bf16[128,1920]{1,0:T(8,128)(2,1)} %get-tuple-element.36), channel_id=1, source_target_pairs={{0,1},{1,0},{2,3},{3,2},{4,5},{5,4},{6,7},{7,6},{8,9},{9,8},{10,11... | collective-permute-start | bytes 1474568 | tf_op jit(solution)/shard_map/ppermute | solution.py:33
  124.6 26.9 %all-to-all-start.2 = ((bf16[8,176,128]{2,1,0:T(8,128)(2,1)}), bf16[8,176,128]{2,1,0:T(8,128)(2,1)S(1)}, u32[]{:S(2)}, u32[]{:S(2)}) async-start(bf16[8,176,128]{2,1,0:T(8,128)(2,1)} %pad_maximum_fusion.3), calls=%async_computation.2 | async-start | bytes 720896 | tf_op jit(solution)/shard_map/all_to_all | solution.py:37
  146.4 38.9 %collective-permute-start.13 = (bf16[1920,128]{1,0:T(8,128)(2,1)}, bf16[1920,128]{1,0:T(8,128)(2,1)}, u32[]{:S(2)}, u32[]{:S(2)}) collective-permute-start(bf16[1920,128]{1,0:T(8,128)(2,1)} %convolution_convert_fusion.2), channel_id=1, source_target_pairs={{0,32},{32,64},{64,96},{96,0},{1,33},{33,65},{65,97},{97,1},{2,34}... | collective-permute-start | bytes 1474568 | tf_op jit(solution)/shard_map/ppermute | solution.py:533
  147.8 37.6 %collective-permute-start.14 = (bf16[1920,128]{1,0:T(8,128)(2,1)}, bf16[1920,128]{1,0:T(8,128)(2,1)}, u32[]{:S(2)}, u32[]{:S(2)}) collective-permute-start(bf16[1920,128]{1,0:T(8,128)(2,1)} %convolution_convert_fusion.1), channel_id=1, source_target_pairs={{0,64},{32,96},{64,0},{96,32},{1,65},{33,97},{65,1},{97,33},{2,66}... | collective-permute-start | bytes 1474568 | tf_op jit(solution)/shard_map/ppermute | solution.py:533
  150.4 35.0 %collective-permute-start.15 = (bf16[1920,128]{1,0:T(8,128)(2,1)}, bf16[1920,128]{1,0:T(8,128)(2,1)}, u32[]{:S(2)}, u32[]{:S(2)}) collective-permute-start(bf16[1920,128]{1,0:T(8,128)(2,1)} %convolution_convert_fusion), channel_id=1, source_target_pairs={{0,96},{32,0},{64,32},{96,64},{1,97},{33,1},{65,33},{97,65},{2,98}... | collective-permute-start | bytes 1474568 | tf_op jit(solution)/shard_map/ppermute | solution.py:533
  163.2 2.0 collective-permute-start.16
  165.2 7.6 %collective-permute-start.17 = (f32[48,128]{1,0:T(8,128)S(1)}, f32[48,128]{1,0:T(8,128)S(1)}, u32[]{:S(2)}, u32[]{:S(2)}) collective-permute-start(f32[48,128]{1,0:T(8,128)S(1)} %add.110), channel_id=1, source_target_pairs={{0,64},{32,96},{64,0},{96,32},{1,65},{33,97},{65,1},{97,33},{2,66}... | collective-permute-start | bytes 73736 | tf_op jit(solution)/shard_map/ppermute | solution.py:542
  167.9 14.8 %collective-permute-start.18 = (f32[48,128]{1,0:T(8,128)S(1)}, f32[48,128]{1,0:T(8,128)S(1)}, u32[]{:S(2)}, u32[]{:S(2)}) collective-permute-start(f32[48,128]{1,0:T(8,128)S(1)} %add.110), channel_id=1, source_target_pairs={{0,32},{32,64},{64,96},{96,0},{1,33},{33,65},{65,97},{97,1},{2,34}... | collective-permute-start | bytes 73736 | tf_op jit(solution)/shard_map/ppermute | solution.py:542
  172.8 12.5 %collective-permute-start.19 = (f32[48,128]{1,0:T(8,128)S(1)}, f32[48,128]{1,0:T(8,128)S(1)}, u32[]{:S(2)}, u32[]{:S(2)}) collective-permute-start(f32[48,128]{1,0:T(8,128)S(1)} %add.110), channel_id=1, source_target_pairs={{0,96},{32,0},{64,32},{96,64},{1,97},{33,1},{65,33},{97,65},{2,98}... | collective-permute-start | bytes 73736 | tf_op jit(solution)/shard_map/ppermute | solution.py:542
  174.0 18.9 %all-to-all-start.3 = ((bf16[8,128,128]{2,1,0:T(8,128)(2,1)}), bf16[8,128,128]{2,1,0:T(8,128)(2,1)}, u32[]{:S(2)}, u32[]{:S(2)}) async-start(bf16[8,128,128]{2,1,0:T(8,128)(2,1)} %bitcast.21), calls=%async_computation.3 | async-start | bytes 524288 | tf_op jit(solution)/shard_map/all_to_all | solution.py:37
  182.7 10.5 %collective-permute-start.9 = (bf16[2,2,512,256]{3,2,1,0:T(8,128)(2,1)S(1)}, bf16[2,2,512,256]{3,2,1,0:T(8,128)(2,1)}, u32[]{:S(2)}, u32[]{:S(2)}) collective-permute-start(bf16[2,2,512,256]{3,2,1,0:T(8,128)(2,1)S(1)} %get-tuple-element.41), channel_id=1, source_target_pairs={{0,1},{1,0},{2,3},{3,2},{4,5},{5,4},{6,7},{7,6},{8,9},{9,8},{10,11... | collective-permute-start | bytes 3145736 | tf_op jit(solution)/shard_map/ppermute | solution.py:33
  194.8 19.7 %collective-permute-start.10 = (bf16[2,512,256]{2,1,0:T(8,128)(2,1)S(1)}, bf16[2,512,256]{2,1,0:T(8,128)(2,1)}, u32[]{:S(2)}, u32[]{:S(2)}) collective-permute-start(bf16[2,512,256]{2,1,0:T(8,128)(2,1)S(1)} %fusion.7), channel_id=1, source_target_pairs={{0,8},{8,0},{1,9},{9,1},{2,10},{10,2},{3,11},{11,3},{4,12},{12,4},... | collective-permute-start | bytes 1572872 | tf_op jit(solution)/shard_map/ppermute | solution.py:33
  195.1 10.7 %collective-permute-start.20 = (bf16[528,128]{1,0:T(8,128)(2,1)S(1)}, bf16[528,128]{1,0:T(8,128)(2,1)S(1)}, u32[]{:S(2)}, u32[]{:S(2)}) collective-permute-start(bf16[528,128]{1,0:T(8,128)(2,1)S(1)} %get-tuple-element.83), channel_id=1, source_target_pairs={{0,0},{1,128},{8,8},{9,136},{128,1},{129,129},{136,9},{137,137},{2... | collective-permute-start | bytes 405512 | tf_op jit(solution)/shard_map/ppermute | solution.py:568
  202.7 5.7 %collective-permute-start.21 = (bf16[528,128]{1,0:T(8,128)(2,1)S(1)}, bf16[528,128]{1,0:T(8,128)(2,1)S(1)}, u32[]{:S(2)}, u32[]{:S(2)}) collective-permute-start(bf16[528,128]{1,0:T(8,128)(2,1)S(1)} %get-tuple-element.84), channel_id=1, source_target_pairs={{0,8},{1,136},{8,0},{9,128},{128,9},{129,137},{136,1},{137,129},{2... | collective-permute-start | bytes 405512 | tf_op jit(solution)/shard_map/ppermute | solution.py:568
  204.3 4.1 %collective-permute-start.22 = (bf16[528,128]{1,0:T(8,128)(2,1)S(1)}, bf16[528,128]{1,0:T(8,128)(2,1)S(1)}, u32[]{:S(2)}, u32[]{:S(2)}) collective-permute-start(bf16[528,128]{1,0:T(8,128)(2,1)S(1)} %get-tuple-element.85), channel_id=1, source_target_pairs={{0,1},{1,129},{8,9},{9,137},{128,0},{129,128},{136,8},{137,136},{2... | collective-permute-start | bytes 405512 | tf_op jit(solution)/shard_map/ppermute | solution.py:568
  204.3 10.1 %collective-permute-start.23 = (bf16[528,128]{1,0:T(8,128)(2,1)S(1)}, bf16[528,128]{1,0:T(8,128)(2,1)S(1)}, u32[]{:S(2)}, u32[]{:S(2)}) collective-permute-start(bf16[528,128]{1,0:T(8,128)(2,1)S(1)} %get-tuple-element.86), channel_id=1, source_target_pairs={{0,9},{1,137},{8,1},{9,129},{128,8},{129,136},{136,0},{137,128},{2... | collective-permute-start | bytes 405512 | tf_op jit(solution)/shard_map/ppermute | solution.py:568
  216.8 27.3 %all-to-all-start.4 = ((bf16[8,364,128]{2,1,0:T(8,128)(2,1)}), bf16[8,364,128]{2,1,0:T(8,128)(2,1)S(1)}, u32[]{:S(2)}, u32[]{:S(2)}) async-start(bf16[8,364,128]{2,1,0:T(8,128)(2,1)} %pad_maximum_fusion.2), calls=%async_computation.4 | async-start | bytes 1507328 | tf_op jit(solution)/shard_map/all_to_all | solution.py:37
  (18 other events, 161.0 us)
